TPU v7x, 512 devices: a whole 4x8x8 slice. The times are simulated.
512 devices in a mesh: frames: 64 (over y_hi, z, core), rows: 8 (over x, y_lo).
Axes of the slice: x: 4, y: 8 (y_hi: 4, y_lo: 2; y = y_hi * 2 + y_lo), z: 8, core: 2. Of those that a mesh axis runs over, the one named last changes fastest.
Arguments:
- tokens: bfloat16 [64, 128, 16, 256], P('frames', 'rows'), may hold values from -6 to 6
- keep_mask: int32 [64, 128, 16], P('frames'), may hold values 0 or 1
- gain_two: float32 [256], replicated, may hold values from 0.1 to 1.9
- attend_two: bfloat16 [256, 768], replicated, may hold values from -0.375 to 0.375
- scale_two: float32 [4], replicated, may hold values from 2 to 8
- output_two: bfloat16 [256, 256], replicated, may hold values from -0.375 to 0.375
- merge_weight: bfloat16 [1024, 512], replicated, may hold values from -0.1875 to 0.1875
- gain_three: float32 [512], replicated, may hold values from 0.1 to 1.9
- attend_three: bfloat16 [512, 1536], replicated, may hold values from -0.25 to 0.25
- scale_three: float32 [8], replicated, may hold values from 2 to 8
- output_three: bfloat16 [512, 512], replicated, may hold values from -0.25 to 0.25
- cotangent: bfloat16 [64, 64, 8, 512], P('frames', 'rows'), may hold values from -6 to 6
Outputs:
- tokens_grad: bfloat16 [64, 128, 16, 256], P('frames', 'rows')
- weight_grads: float32 [512, 1024], P(('frames', 'rows'))
Inputs may be any that keep to these rules, and one draw needn't show every extreme that they name: `keep_mask`: 1 where a patch is valid, 0 where it is padding.
All inputs are finite; a program needn't handle non-finite values. No bound on the sum of `keep_mask` on one device may be relied on, other than what follows from the above.
Results may differ from a plain program's by a relative error of at most 0.019.
Values may be sent and summed in bfloat16 or wider, within the bound.
No kernel may reach another device: no remote copies, remote signals or barrier semaphores. Data moves between devices by JAX's collectives and lax.ppermute only.
A program may use at most 64 MiB of HBM per device.

v0:
```python
import jax
import jax.numpy as jnp
from jax import lax
from jax.sharding import PartitionSpec as P

HEAD = 64


epsilon = 1e-06


def extended(cells, sides, width):
    for axis, dim in sides:
        count = lax.axis_size(axis)
        ends = count - 1
        head = lax.slice_in_dim(cells, 0, width, axis=dim)
        tail = lax.slice_in_dim(cells, cells.shape[dim] - width, cells.shape[dim], axis=dim)
        cells = jnp.concatenate(
            [
                lax.ppermute(tail, axis, [(i, (i + 1) % count) for i in range(ends)]),
                cells,
                lax.ppermute(head, axis, [((i + 1) % count, i) for i in range(ends)]),
            ],
            axis=dim,
        )
    return cells


def float_dot(left, right):
    return jnp.dot(left, right, preferred_element_type=jnp.float32, precision=lax.Precision.HIGHEST)


def project(left, right):
    return float_dot(left, right).astype(jnp.bfloat16)


def scaled_norm(values, gain):
    return (
        values * lax.rsqrt(jnp.mean(values * values, axis=-1, keepdims=True) + epsilon) * gain
    ).astype(jnp.bfloat16)


def cosine_heads(triple, scale, head):
    width = triple.shape[-1] // 3
    count = triple.shape[0]
    heads = width // head
    query = triple[:, :width].astype(jnp.float32).reshape(count, heads, head)
    keys = triple[:, width : 2 * width].astype(jnp.float32).reshape(count, heads, head)
    query = (
        query * lax.rsqrt(jnp.sum(query * query, axis=-1, keepdims=True) + epsilon) * scale[:, None]
    )
    keys = keys * lax.rsqrt(jnp.sum(keys * keys, axis=-1, keepdims=True) + epsilon)
    query = query.reshape(count, width).astype(jnp.bfloat16)
    keys = keys.reshape(count, width).astype(jnp.bfloat16)
    return (query, jnp.concatenate([keys, triple[:, 2 * width :]], axis=-1))


def tile_masks():
    query_pos = jnp.arange(64)
    key_pos = jnp.arange(196)
    down = key_pos[None, :] // 14 - query_pos[:, None] // 8
    across = key_pos[None, :] % 14 - query_pos[:, None] % 8
    inside = ((down >= 0) & (down <= 6) & (across >= 0) & (across <= 6)).astype(jnp.float32)
    centre = ((down == 3) & (across == 3)).astype(jnp.float32)
    return (inside, centre)


def neighbour_attention(query, padded, allow_pad, head):
    frames, rows, cols, width = query.shape
    heads = width // head
    row_tiles = rows // 8
    col_tiles = cols // 8
    blocks = query.reshape(frames, row_tiles, 8, col_tiles, 8, heads, head)
    blocks = blocks.transpose(0, 1, 3, 5, 2, 4, 6).reshape(
        frames, row_tiles, col_tiles, heads, 64, head
    )
    windows = jnp.stack(
        [
            jnp.stack(
                [
                    padded[:, 8 * row_tile : 8 * row_tile + 14, 8 * col_tile : 8 * col_tile + 14]
                    for col_tile in range(col_tiles)
                ],
                1,
            )
            for row_tile in range(row_tiles)
        ],
        1,
    )
    allowed = jnp.stack(
        [
            jnp.stack(
                [
                    allow_pad[:, 8 * row_tile : 8 * row_tile + 14, 8 * col_tile : 8 * col_tile + 14]
                    for col_tile in range(col_tiles)
                ],
                1,
            )
            for row_tile in range(row_tiles)
        ],
        1,
    )
    allowed = allowed.reshape(frames, row_tiles, col_tiles, 1, 1, 196)
    windows = windows.reshape(frames, row_tiles, col_tiles, 196, 2, heads, head).astype(
        jnp.bfloat16
    )
    inside, centre = tile_masks()
    scores = jnp.einsum(
        "ftcqhd,ftckhd->ftchqk",
        blocks.transpose(0, 1, 2, 4, 3, 5),
        windows[:, :, :, :, 0],
        preferred_element_type=jnp.float32,
    )
    weights = jnp.exp(scores) * (inside * jnp.maximum(allowed, centre))
    probs = (weights / jnp.sum(weights, axis=-1, keepdims=True)).astype(jnp.bfloat16)
    result = jnp.einsum(
        "ftchqk,ftckhd->ftchqd", probs, windows[:, :, :, :, 1], preferred_element_type=jnp.float32
    )
    result = result.reshape(frames, row_tiles, col_tiles, heads, 8, 8, head).transpose(
        0, 1, 4, 2, 5, 3, 6
    )
    return result.reshape(frames, rows, cols, width).astype(jnp.bfloat16)


def frame_attention(query, keyval, head):
    frames, places, width = query.shape
    heads = width // head
    queries = query.reshape(frames, places, heads, head)
    keys = keyval[:, :, :width].reshape(frames, places, heads, head)
    values = keyval[:, :, width:].reshape(frames, places, heads, head)
    scores = jnp.einsum("flhd,glhd->lhfg", queries, keys, preferred_element_type=jnp.float32)
    weights = jnp.exp(scores)
    probs = (weights / jnp.sum(weights, axis=-1, keepdims=True)).astype(jnp.bfloat16)
    result = jnp.einsum("lhfg,glhd->flhd", probs, values, preferred_element_type=jnp.float32)
    return result.reshape(frames, places, width).astype(jnp.bfloat16)


def patch_merge(grid):
    frames, rows, cols, width = grid.shape
    merged = grid.reshape(frames, rows // 2, 2, cols // 2, 2, width).transpose(0, 1, 3, 2, 4, 5)
    return merged.reshape(frames * (rows // 2) * (cols // 2), 4 * width)


def coarse_forward(merged_wide, gain_three, attend_three, scale_three):
    normed_three, norm_three_back = jax.vjp(
        lambda value: scaled_norm(value, gain_three), merged_wide
    )
    triple_three, proj_three_back = jax.vjp(
        lambda value: project(value, attend_three), normed_three
    )
    (query_three, keyval_three), heads_three_back = jax.vjp(
        lambda value: cosine_heads(value, scale_three, HEAD), triple_three
    )
    return (query_three, keyval_three, norm_three_back, proj_three_back, heads_three_back)


def body(
    tokens,
    keep_mask,
    gain_two,
    attend_two,
    scale_two,
    output_two,
    merge_weight,
    gain_three,
    attend_three,
    scale_three,
    output_three,
    cotangent,
):
    frames, rows, cols, width = tokens.shape
    wide = output_three.shape[0]
    parts = lax.axis_size("frames")
    places = rows // 2 * (cols // 2) // parts
    widened = tokens.astype(jnp.float32).reshape(-1, width)
    normed_two, norm_two_back = jax.vjp(lambda value: scaled_norm(value, gain_two), widened)
    triple_two, proj_two_back = jax.vjp(lambda value: project(value, attend_two), normed_two)
    (query_two, keyval_two), heads_two_back = jax.vjp(
        lambda value: cosine_heads(value, scale_two, HEAD), triple_two
    )
    grid_keyval = keyval_two.reshape(frames, rows, cols, 2 * width)
    band = extended(grid_keyval, (("rows", 1),), 3)
    padded = jnp.pad(band.astype(jnp.float32), ((0, 0), (0, 0), (3, 3), (0, 0)))
    keep_pad = jnp.pad(keep_mask.astype(jnp.float32), ((0, 0), (3, 3), (3, 3)))
    allow_pad = lax.dynamic_slice_in_dim(keep_pad, lax.axis_index("rows") * rows, rows + 6, 1)
    attn_grid, neighbour_back = jax.vjp(
        lambda query, keyval: neighbour_attention(query, keyval, allow_pad, HEAD),
        query_two.reshape(frames, rows, cols, width),
        padded,
    )
    attn_two = attn_grid.reshape(-1, width)
    mixed_two = (widened + float_dot(attn_two, output_two)).astype(jnp.bfloat16)
    merged, merge_back = jax.vjp(
        lambda value: project(patch_merge(value), merge_weight),
        mixed_two.reshape(frames, rows, cols, width),
    )
    target = cotangent.reshape(-1, wide)
    merged_wide = merged.astype(jnp.float32)
    query_three, keyval_three, norm_three_back, proj_three_back, heads_three_back = coarse_forward(
        merged_wide, gain_three, attend_three, scale_three
    )
    triple = jnp.concatenate([query_three, keyval_three], axis=-1).reshape(
        frames, parts, places, 3 * wide
    )
    placed = lax.all_to_all(triple, "frames", split_axis=1, concat_axis=0, tiled=True)
    attn_place, place_back = jax.vjp(
        lambda query, keyval: frame_attention(query, keyval, HEAD),
        placed[:, 0, :, :wide],
        placed[:, 0, :, wide:],
    )
    attn_three = lax.all_to_all(
        attn_place[:, None], "frames", split_axis=0, concat_axis=1, tiled=True
    ).reshape(-1, wide)
    grad_out_three = float_dot(attn_three.T, target)
    target_wide = target.astype(jnp.float32)
    ct_attn_three = jax.vjp(lambda value: float_dot(value, output_three), attn_three)[1](
        target_wide
    )[0]
    ct_place = lax.all_to_all(
        ct_attn_three.reshape(frames, parts, places, wide),
        "frames",
        split_axis=1,
        concat_axis=0,
        tiled=True,
    )
    ct_query_place, ct_keyval_place = place_back(ct_place[:, 0])
    ct_triple = lax.all_to_all(
        jnp.concatenate([ct_query_place, ct_keyval_place], axis=-1)[:, None],
        "frames",
        split_axis=0,
        concat_axis=1,
        tiled=True,
    ).reshape(-1, 3 * wide)
    ct_triple_three = heads_three_back((ct_triple[:, :wide], ct_triple[:, wide:]))[0]
    ct_merged_wide = target_wide + norm_three_back(proj_three_back(ct_triple_three)[0])[0]
    ct_merged = ct_merged_wide.astype(jnp.bfloat16)
    ct_mixed = merge_back(ct_merged)[0].reshape(-1, width)
    grad_out_two = float_dot(attn_two.T, ct_mixed)
    ct_widened = ct_mixed.astype(jnp.float32)
    ct_attn_two = jax.vjp(lambda value: float_dot(value, output_two), attn_two)[1](ct_widened)[0]
    ct_query_two, ct_padded = neighbour_back(ct_attn_two.reshape(frames, rows, cols, width))
    ct_band = ct_padded[:, :, 3 : cols + 3]
    edges = jnp.concatenate([ct_band[:, :3], ct_band[:, rows + 3 :]], axis=1)
    beside_all = extended(edges.astype(jnp.bfloat16), (("rows", 1),), 3).astype(edges.dtype)
    inner = ct_band[:, 3 : rows + 3]
    inner = jnp.concatenate(
        [
            inner[:, :3] + beside_all[:, :3],
            inner[:, 3 : rows - 3],
            inner[:, rows - 3 :] + beside_all[:, 9:],
        ],
        axis=1,
    )
    ct_keyval_two = inner.astype(jnp.bfloat16).reshape(-1, 2 * width)
    ct_triple_two = heads_two_back((ct_query_two.reshape(-1, width), ct_keyval_two))[0]
    grad_attend_two = float_dot(normed_two.T, ct_triple_two)
    ct_widened = ct_widened + norm_two_back(proj_two_back(ct_triple_two)[0])[0]
    tokens_grad = ct_widened.astype(jnp.bfloat16).reshape(frames, rows, cols, width)
    devices = parts * lax.axis_size("rows")
    flat = jnp.concatenate(
        [grad_attend_two.reshape(-1), grad_out_two.reshape(-1), grad_out_three.reshape(-1)]
    ).reshape(devices, -1)
    shards = lax.psum_scatter(flat, ("frames", "rows"), scatter_dimension=0, tiled=True)
    return (tokens_grad, shards)


def solution(mesh):
    return jax.shard_map(
        body,
        mesh=mesh,
        in_specs=(
            P("frames", "rows", None, None),
            P("frames", None, None),
            P(),
            P(),
            P(),
            P(),
            P(),
            P(),
            P(),
            P(),
            P(),
            P("frames", "rows", None, None),
        ),
        out_specs=(P("frames", "rows", None, None), P(("frames", "rows"), None)),
        check_vma=False,
    )
```

profile of v0, /device:TPU:1, one launch (start us, length us, event | category | flops | bytes accessed | tf_op | source)
XLA Modules:
  0.0 533.2 jit_solution(5686106904272919820)
XLA Ops:
  15.3 4.0 collective-permute-start
  23.2 16.4 %all-to-all-start = ((bf16[64,2,256]{2,1,0:T(2,128)(2,1)}), bf16[64,2,256]{2,1,0:T(2,128)(2,1)}, u32[]{:S(2)}, u32[]{:S(2)}) async-start(bf16[64,2,256]{2,1,0:T(2,128)(2,1)} %reshape.889), calls=%async_computation | async-start | bytes 131072 | tf_op jit(solution)/shard_map/all_to_all | solution.py:219
  67.9 3.4 reduce.9
  72.9 12.9 %all-to-all-start.1 = ((bf16[64,2,768]{2,1,0:T(2,128)(2,1)}), bf16[64,2,768]{2,1,0:T(2,128)(2,1)}, u32[]{:S(2)}, u32[]{:S(2)}) async-start(bf16[64,2,768]{2,1,0:T(2,128)(2,1)} %reshape.887), calls=%async_computation.1 | async-start | bytes 393216 | tf_op jit(solution)/shard_map/all_to_all | solution.py:205
  89.0 9.7 %all-to-all-done.1 = bf16[64,2,768]{2,1,0:T(2,128)(2,1)} async-done(((bf16[64,2,768]{2,1,0:T(2,128)(2,1)}), bf16[64,2,768]{2,1,0:T(2,128)(2,1)}, u32[]{:S(2)}, u32[]{:S(2)}) %all-to-all-start.1) | async-done | bytes 196640 | tf_op jit(solution)/shard_map/all_to_all | solution.py:205
  98.7 2.2 reshape.888
  106.5 1.9 fusion.92
  111.2 1.9 convolution_convert_fusion.14
  123.8 2.2 reduce.12
  129.1 5.5 %all-to-all-start.3 = ((bf16[64,2,256]{2,1,0:T(2,128)(2,1)}), bf16[64,2,256]{2,1,0:T(2,128)(2,1)}, u32[]{:S(2)}, u32[]{:S(2)}) async-start(bf16[64,2,256]{2,1,0:T(2,128)(2,1)} %reshape.893), calls=%async_computation.3 | async-start | bytes 131072 | tf_op jit(solution)/shard_map/all_to_all | solution.py:211
  137.1 2.3 reduce.11
  141.0 5.5 %all-to-all-done.3 = bf16[64,2,256]{2,1,0:T(2,128)(2,1)} async-done(((bf16[64,2,256]{2,1,0:T(2,128)(2,1)}), bf16[64,2,256]{2,1,0:T(2,128)(2,1)}, u32[]{:S(2)}, u32[]{:S(2)}) %all-to-all-start.3) | async-done | bytes 65568 | tf_op jit(solution)/shard_map/all_to_all | solution.py:211
  146.6 7.4 %all-to-all-start.2 = ((bf16[64,2,768]{2,1,0:T(2,128)(2,1)}), bf16[64,2,768]{2,1,0:T(2,128)(2,1)}, u32[]{:S(2)}, u32[]{:S(2)}) async-start(bf16[64,2,768]{2,1,0:T(2,128)(2,1)} %reshape.891), calls=%async_computation.2 | async-start | bytes 393216 | tf_op jit(solution)/shard_map/all_to_all | solution.py:227
  158.6 8.2 %all-to-all-done.2 = bf16[64,2,768]{2,1,0:T(2,128)(2,1)} async-done(((bf16[64,2,768]{2,1,0:T(2,128)(2,1)}), bf16[64,2,768]{2,1,0:T(2,128)(2,1)}, u32[]{:S(2)}, u32[]{:S(2)}) %all-to-all-start.2) | async-done | bytes 196640 | tf_op jit(solution)/shard_map/all_to_all | solution.py:227
  166.8 2.2 reshape.892
  187.8 1.9 fusion
  193.7 4.7 copy.203
  198.4 4.1 reshape.881
  214.3 5.6 %collective-permute-start.2 = (bf16[1,3,16,512]{3,2,1,0:T(8,128)(2,1)}, bf16[1,3,16,512]{3,2,1,0:T(8,128)(2,1)}, u32[]{:S(2)}, u32[]{:S(2)}) collective-permute-start(bf16[1,3,16,512]{3,2,1,0:T(8,128)(2,1)} %copy.275), channel_id=1, source_target_pairs={{0,1},{1,2},{2,3},{3,4},{4,5},{5,6},{6,7},{8,9},{9,10},{10,11},{11... | collective-permute-start | bytes 147464 | tf_op jit(solution)/shard_map/ppermute | solution.py:20
  220.7 2.0 slice.196
  226.4 2.1 reshape.882
  244.5 2.4 pad_maximum_fusion
  246.9 2.7 reshape.879
  252.1 272.9 %all-reduce.19.cloned.1.call-done = f32[512,1024]{1,0:T(8,128)} async-done(((f32[512,1024]{1,0:T(8,128)}), f32[512,1024]{1,0:T(8,128)}) %all-reduce.19.cloned.1.call-update) | async-done | bytes 2097168
  (317 shorter events, 133.7 us)
Async XLA Ops:
  7.2 44.9 %copy-start = (bf16[512,1536]{1,0:T(8,128)(2,1)S(1)}, bf16[512,1536]{1,0:T(8,128)(2,1)}, u32[]{:S(2)}) copy-start(bf16[512,1536]{1,0:T(8,128)(2,1)} %param.20) | copy-start | bytes 4718596
  13.7 6.9 %copy-start.30 = (bf16[1,8,8,512]{3,2,1,0:T(8,128)(2,1)S(1)}, bf16[1,8,8,512]{3,2,1,0:T(8,128)(2,1)}, u32[]{:S(2)}) copy-start(bf16[1,8,8,512]{3,2,1,0:T(8,128)(2,1)} %param.23) | copy-start | bytes 196612
  13.8 6.9 %copy-start.35 = (bf16[512,512]{1,0:T(8,128)(2,1)S(1)}, bf16[512,512]{1,0:T(8,128)(2,1)}, u32[]{:S(2)}) copy-start(bf16[512,512]{1,0:T(8,128)(2,1)} %param.22) | copy-start | bytes 1572868
  14.1 25.7 %copy-start.13 = (f32[256,256]{1,0:T(8,128)}, f32[256,256]{1,0:T(8,128)S(1)}, u32[]{:S(2)}) copy-start(f32[256,256]{1,0:T(8,128)S(1)} %copy.176) | copy-start | bytes 786436
  14.1 25.5 %copy-start.55 = (s32[1,128,16]{1,2,0:T(8,128)S(1)}, s32[1,128,16]{1,2,0:T(8,128)}, u32[]{:S(2)}) copy-start(s32[1,128,16]{1,2,0:T(8,128)} %param.13) | copy-start | bytes 24580
  14.4 26.5 %copy-start.59 = (f32[8]{0:T(128)S(1)}, f32[8]{0:T(128)}, u32[]{:S(2)}) copy-start(f32[8]{0:T(128)} %param.21) | copy-start | bytes 100
  15.3 26.3 %collective-permute-start = (bf16[1,3,16,512]{3,2,1,0:T(8,128)(2,1)S(1)}, bf16[1,3,16,512]{3,2,1,0:T(8,128)(2,1)S(1)}, u32[]{:S(2)}, u32[]{:S(2)}) collective-permute-start(bf16[1,3,16,512]{3,2,1,0:T(8,128)(2,1)S(1)} %get-tuple-element.26), channel_id=1, source_target_pairs={{0,1},{1,2},{2,3},{3,4},{4,5},{5,6},{6,7},{8,9},{9,10},{10,11},{11... | collective-permute-start | bytes 147464 | tf_op jit(solution)/shard_map/ppermute | solution.py:20
  19.4 22.2 %collective-permute-start.1 = (bf16[1,3,16,512]{3,2,1,0:T(8,128)(2,1)S(1)}, bf16[1,3,16,512]{3,2,1,0:T(8,128)(2,1)S(1)}, u32[]{:S(2)}, u32[]{:S(2)}) collective-permute-start(bf16[1,3,16,512]{3,2,1,0:T(8,128)(2,1)S(1)} %get-tuple-element.27), channel_id=1, source_target_pairs={{1,0},{2,1},{3,2},{4,3},{5,4},{6,5},{7,6},{9,8},{10,9},{11,10},{12... | collective-permute-start | bytes 147464 | tf_op jit(solution)/shard_map/ppermute | solution.py:22
  23.2 49.7 %all-to-all-start = ((bf16[64,2,256]{2,1,0:T(2,128)(2,1)}), bf16[64,2,256]{2,1,0:T(2,128)(2,1)}, u32[]{:S(2)}, u32[]{:S(2)}) async-start(bf16[64,2,256]{2,1,0:T(2,128)(2,1)} %reshape.889), calls=%async_computation | async-start | bytes 131072 | tf_op jit(solution)/shard_map/all_to_all | solution.py:219
  40.9 6.8 %copy-start.28 = (bf16[1,2,8,2,8,4,64]{6,5,4,3,2,1,0:T(4,128)(2,1)}, bf16[1,2,8,2,8,4,64]{6,5,4,3,2,1,0:T(4,128)(2,1)S(1)}, u32[]{:S(2)}) copy-start(bf16[1,2,8,2,8,4,64]{6,5,4,3,2,1,0:T(4,128)(2,1)S(1)} %reshape_reshape.6) | copy-start | bytes 393220
  72.9 25.8 %all-to-all-start.1 = ((bf16[64,2,768]{2,1,0:T(2,128)(2,1)}), bf16[64,2,768]{2,1,0:T(2,128)(2,1)}, u32[]{:S(2)}, u32[]{:S(2)}) async-start(bf16[64,2,768]{2,1,0:T(2,128)(2,1)} %reshape.887), calls=%async_computation.1 | async-start | bytes 393216 | tf_op jit(solution)/shard_map/all_to_all | solution.py:205
  129.1 17.5 %all-to-all-start.3 = ((bf16[64,2,256]{2,1,0:T(2,128)(2,1)}), bf16[64,2,256]{2,1,0:T(2,128)(2,1)}, u32[]{:S(2)}, u32[]{:S(2)}) async-start(bf16[64,2,256]{2,1,0:T(2,128)(2,1)} %reshape.893), calls=%async_computation.3 | async-start | bytes 131072 | tf_op jit(solution)/shard_map/all_to_all | solution.py:211
  146.6 20.3 %all-to-all-start.2 = ((bf16[64,2,768]{2,1,0:T(2,128)(2,1)}), bf16[64,2,768]{2,1,0:T(2,128)(2,1)}, u32[]{:S(2)}, u32[]{:S(2)}) async-start(bf16[64,2,768]{2,1,0:T(2,128)(2,1)} %reshape.891), calls=%async_computation.2 | async-start | bytes 393216 | tf_op jit(solution)/shard_map/all_to_all | solution.py:227
  153.9 371.1 %all-reduce.19.cloned.1.call-start = ((), (), s32[]{:S(2)}) async-start(), calls=%async_computation.4 | async-start | bytes 4194304
  174.4 9.5 %copy-start.19 = (bf16[64,1,1,1536]{3,0,1,2:T(8,128)(2,1)S(1)}, bf16[64,1,1,1536]{3,0,1,2:T(8,128)(2,1)}, u32[]{:S(2)}) copy-start(bf16[64,1,1,1536]{3,0,1,2:T(8,128)(2,1)} %copy-done.18) | copy-start | bytes 589828
  205.2 7.1 %copy-start.39 = (f32[1,2,2,4,8,8,64]{6,5,4,3,2,1,0:T(8,128)S(1)}, f32[1,2,2,4,8,8,64]{6,5,4,3,2,1,0:T(8,128)}, u32[]{:S(2)}) copy-start(f32[1,2,2,4,8,8,64]{6,5,4,3,2,1,0:T(8,128)} %fusion.4) | copy-start | bytes 786436
  206.2 6.9 %copy-start.61 = (f32[4]{0:T(128)S(1)}, f32[4]{0:T(128)}, u32[]{:S(2)}) copy-start(f32[4]{0:T(128)} %param.16) | copy-start | bytes 52
  210.0 21.3 %collective-permute-start.3 = (bf16[1,3,16,512]{3,0,2,1:T(2,128)(2,1)}, bf16[1,3,16,512]{3,0,2,1:T(2,128)(2,1)}, u32[]{:S(2)}, u32[]{:S(2)}) collective-permute-start(bf16[1,3,16,512]{3,0,2,1:T(2,128)(2,1)} %get-tuple-element.5), channel_id=1, source_target_pairs={{1,0},{2,1},{3,2},{4,3},{5,4},{6,5},{7,6},{9,8},{10,9},{11,10},{12... | collective-permute-start | bytes 147464 | tf_op jit(solution)/shard_map/ppermute | solution.py:22
  214.3 16.1 %collective-permute-start.2 = (bf16[1,3,16,512]{3,2,1,0:T(8,128)(2,1)}, bf16[1,3,16,512]{3,2,1,0:T(8,128)(2,1)}, u32[]{:S(2)}, u32[]{:S(2)}) collective-permute-start(bf16[1,3,16,512]{3,2,1,0:T(8,128)(2,1)} %copy.275), channel_id=1, source_target_pairs={{0,1},{1,2},{2,3},{3,4},{4,5},{5,6},{6,7},{8,9},{9,10},{10,11},{11... | collective-permute-start | bytes 147464 | tf_op jit(solution)/shard_map/ppermute | solution.py:20
  233.4 6.8 %copy-start.12 = (f32[256,256]{1,0:T(8,128)S(1)}, f32[256,256]{1,0:T(8,128)}, u32[]{:S(2)}) copy-start(f32[256,256]{1,0:T(8,128)} %copy-done.11) | copy-start | bytes 786436
  233.4 6.8 %copy-start.14 = (f32[256,256]{1,0:T(8,128)S(1)}, f32[256,256]{1,0:T(8,128)}, u32[]{:S(2)}) copy-start(f32[256,256]{1,0:T(8,128)} %copy-done.13) | copy-start | bytes 786436
  233.4 6.8 %copy-start.50 = (f32[256]{0:T(256)S(1)}, f32[256]{0:T(256)}, u32[]{:S(2)}) copy-start(f32[256]{0:T(256)} %copy-done.49) | copy-start | bytes 3076
  233.5 6.8 %copy-start.25 = (f32[256,256]{1,0:T(8,128)S(1)}, f32[256,256]{1,0:T(8,128)}, u32[]{:S(2)}) copy-start(f32[256,256]{1,0:T(8,128)} %reshape.882) | copy-start | bytes 786436
  233.5 6.8 %copy-start.26 = (f32[256,256]{1,0:T(8,128)S(1)}, f32[256,256]{1,0:T(8,128)}, u32[]{:S(2)}) copy-start(f32[256,256]{1,0:T(8,128)} %copy.216) | copy-start | bytes 786436
  (50 other events, 106.2 us)
Sparse Core Ops, SparseCore 0:
  249.8 275.1 all-reduce.18
where the time goes:
time: 536 us; the launch traced here: 533 us
  waiting for transfers between devices  296 us (55%)
  local copies, waits for them, and re-layouts  103 us (19%)
  starting transfers between devices  54.4 us (10%)
  other arithmetic  43.1 us (8%)
  matrix products  20.6 us (4%)
  between operations  15.4 us (3%)
    unnamed x2, waiting for transfers between devices  273 us
    unnamed x151, local copies, waits for them, and re-layouts  30.8 us
    all_to_all x1, starting transfers between devices, body(): lax.all_to_all(ct_attn_three.reshape(frames, parts, places, wide), 'frame...  16.4 us
    all_to_all x1, starting transfers between devices, body(): lax.all_to_all(triple, 'frames', split_axis=1, concat_axis=0, tiled=True)  12.9 us
  transfers between devices with their start and end apart: 9, of which 4 were waited for; matrix products, arithmetic and copies ran while one was open for 12% of the time, Pallas kernels for 0%

commit v1 on v0

v1 whole, which is shorter than its diff:
```python
import jax
import jax.numpy as jnp
from jax import lax
from jax.experimental import pallas as pl
from jax.experimental.pallas import tpu as pltpu
from jax.sharding import PartitionSpec as P

EPS = 1e-06
BF = jnp.bfloat16
F32 = jnp.float32
HALO = 48
VMEM_BYTES = 32 * 1024 * 1024


def mm(left, right):
    return lax.dot_general(left, right, (((1,), (0,)), ((), ())), preferred_element_type=F32)


def mm_nt(left, right):
    return lax.dot_general(left, right, (((1,), (1,)), ((), ())), preferred_element_type=F32)


def mm_tn(left, right):
    return lax.dot_general(left, right, (((0,), (0,)), ((), ())), preferred_element_type=F32)


def iota(shape, dim):
    return lax.broadcasted_iota(jnp.int32, shape, dim)


def zero_one(condition):
    return jnp.where(condition, 1.0, 0.0).astype(BF)


def head_block():
    return zero_one((iota((256, 256), 0) >> 6) == (iota((256, 256), 1) >> 6))


def head_sum(values, block):
    half = values.astype(BF)
    parts = [mm(half[:, at : at + 256], block) for at in range(0, values.shape[1], 256)]
    return parts[0] if len(parts) == 1 else jnp.concatenate(parts, axis=1)


def scale_lanes(scale_ref, heads):
    lane = iota((1, heads * 64), 1) >> 6
    scale = scale_ref[...]
    out = jnp.zeros((1, heads * 64), F32)
    for head in range(heads):
        out = jnp.where(lane == head, scale[:, head : head + 1], out)
    return out


def split_heads(values, heads):
    lane = iota(values.shape, 1) >> 6
    zero = jnp.zeros_like(values)
    return jnp.concatenate([jnp.where(lane == head, values, zero) for head in range(heads)], axis=0)


def join_heads(stacked, heads):
    rows = stacked.shape[0] // heads
    lane = iota((rows, stacked.shape[1]), 1) >> 6
    out = stacked[:rows]
    for head in range(1, heads):
        out = jnp.where(lane == head, stacked[head * rows : (head + 1) * rows], out)
    return out


def rms(values, gain):
    scale = lax.rsqrt(jnp.mean(values * values, axis=-1, keepdims=True) + EPS)
    return (values * scale * gain).astype(BF)


def rms_back(values, gain, ct):
    scale = lax.rsqrt(jnp.mean(values * values, axis=-1, keepdims=True) + EPS)
    ct = ct * gain
    inner = jnp.mean(ct * values, axis=-1, keepdims=True)
    return scale * ct - values * (scale * scale * scale * inner)


def unit(values, block):
    return values * lax.rsqrt(head_sum(values * values, block) + EPS)


def unit_back(values, ct, block):
    scale = lax.rsqrt(head_sum(values * values, block) + EPS)
    return scale * ct - values * (scale * scale * scale * head_sum(ct * values, block))


def ordering(size, target):
    return zero_one(iota((size, target.shape[1]), 0) == target)


def merge_order():
    patch = iota((1, 256), 1)
    group = ((patch >> 3) & 2) + (patch & 1)
    return ordering(256, (group << 6) + ((patch >> 5) << 3) + ((patch >> 1) & 7))


def bits(count):
    return count.bit_length() - 1


def lanes_to_rows(values):
    count, blocks = values.shape[0], values.shape[1] // 128
    stacked = jnp.concatenate([values[:, 128 * j : 128 * j + 128] for j in range(blocks)], axis=0)
    at = iota((1, count * blocks), 1)
    target = ((at & (count - 1)) << bits(blocks)) + (at >> bits(count))
    return mm(ordering(count * blocks, target), stacked).astype(BF)


def rows_to_lanes(values, blocks):
    total = values.shape[0]
    count = total // blocks
    at = iota((1, total), 1)
    target = ((at & (blocks - 1)) << bits(count)) + (at >> bits(blocks))
    stacked = mm(ordering(total, target), values).astype(BF)
    return jnp.concatenate([stacked[count * j : count * j + count] for j in range(blocks)], axis=1)


def fine_project(
    tokens, gain, attend, scale, normed_out, raw_query_out, raw_key_out, query_out, key_out, value_out
):
    normed = rms(tokens[...].astype(F32), gain[...])
    normed_out[...] = normed
    block = head_block()
    triple = mm(normed, attend[...]).astype(BF)
    raw_query_out[...] = triple[:, :256]
    raw_key_out[...] = triple[:, 256:512]
    query = unit(triple[:, :256].astype(F32), block) * scale_lanes(scale, 4)
    query_out[...] = query.astype(BF)
    key_out[...] = unit(triple[:, 256:512].astype(F32), block).astype(BF)
    value_out[...] = triple[:, 512:]


def allowed_tiles(rank, keep):
    cell = iota((384, 128), 0)
    pick_row = zero_one((cell >> 4) + (16 * rank[0] - 3) == iota((384, 128), 1))
    kept = mm_nt(pick_row, keep[...].astype(F32).astype(BF))
    kept = jnp.where((iota((384, 16), 0) & 15) == iota((384, 16), 1), kept, 0.0)
    kept = jnp.sum(kept, axis=1, keepdims=True)
    spot, home = iota((256, 128), 0), iota((256, 128), 1)
    down = (spot >> 4) - (home >> 4) - 3
    across = (spot & 15) - (home & 15)
    inside = jnp.where((jnp.abs(down) <= 3) & (jnp.abs(across) <= 3), 1.0, 0.0)
    centre = jnp.where((down == 0) & (across == 0), 1.0, 0.0)
    return [inside * jnp.maximum(kept[at : at + 256], centre) for at in (0, 128)]


def fine_forward(
    rank,
    above,
    below,
    query,
    own_keys,
    own_value,
    tokens,
    gain,
    attend,
    keep,
    output,
    cotangent,
    merge,
    beside_out,
    raw_out,
    key_out,
    value_out,
    prob_out,
    attn_out,
    place_out,
):
    halo = jnp.concatenate([above[...], below[...]], axis=0).astype(F32)
    normed = rms(halo, gain[...])
    beside_out[...] = normed
    beside = mm(normed, attend[:, 256:]).astype(BF)
    raw_out[...] = beside[:, :256]
    beside_keys = unit(beside[:, :256].astype(F32), head_block()).astype(BF)
    beside_value = beside[:, 256:]
    rest = jnp.zeros((32, 256), BF)
    keys = jnp.concatenate([beside_keys[:HALO], own_keys[...], beside_keys[HALO:], rest], axis=0)
    value = jnp.concatenate(
        [beside_value[:HALO], own_value[...], beside_value[HALO:], rest], axis=0
    )
    key_out[...] = keys
    value_out[...] = value
    tiles = allowed_tiles(rank, keep)
    parts = []
    for tile in range(2):
        at = 128 * tile
        allowed = jnp.concatenate([tiles[tile]] * 4, axis=1)
        score = mm_nt(keys[at : at + 256], split_heads(query[at : at + 128], 4))
        weight = jnp.exp(score) * allowed
        prob = (weight / jnp.sum(weight, axis=0, keepdims=True)).astype(BF)
        prob_out[tile] = prob
        parts.append(join_heads(mm_tn(prob, value[at : at + 256]), 4))
    attn = jnp.concatenate(parts, axis=0).astype(BF)
    attn_out[...] = attn
    mixed = (tokens[...].astype(F32) + mm(attn, output[...])).astype(BF)
    patches = mm(merge_order(), mixed).astype(BF)
    merged = mm(patches[:64], merge[:256])
    for group in range(1, 4):
        merged += mm(patches[64 * group : 64 * group + 64], merge[256 * group : 256 * group + 256])
    both = jnp.concatenate([merged.astype(BF), cotangent[...]], axis=1)
    place_out[...] = lanes_to_rows(both)


def coarse(place, gain, attend, scale, output, grad_out, back_out):
    both = rows_to_lanes(place[...], 8)
    merged, target = both[:, :512].astype(F32), both[:, 512:]
    block = head_block()
    lanes = scale_lanes(scale, 8)
    normed = rms(merged, gain[...])
    triple = mm(normed, attend[...]).astype(BF)
    query_raw, key_raw = triple[:, :512].astype(F32), triple[:, 512:1024].astype(F32)
    value = triple[:, 1024:]
    query = (unit(query_raw, block) * lanes).astype(BF)
    keys = unit(key_raw, block).astype(BF)
    query_heads = split_heads(query, 8)
    weight = jnp.exp(mm_nt(keys, query_heads))
    prob = weight / jnp.sum(weight, axis=0, keepdims=True)
    prob_half = prob.astype(BF)
    attn = join_heads(mm_tn(prob_half, value), 8).astype(BF)
    at = iota((1, 512), 1)
    slot = ((at & 1) << 8) + (((at >> 1) & 7) << 5) + (at >> 4)
    grad = mm_tn(mm_nt(attn, ordering(512, slot)).astype(BF), target).astype(BF)
    grad_out[...] = jnp.concatenate([grad[:256], grad[256:]], axis=1)
    ct_attn = mm_nt(target, output[...]).astype(BF)
    ct_heads = split_heads(ct_attn, 8)
    ct_prob = mm_nt(value, ct_heads)
    ct_score = prob * (ct_prob - jnp.sum(ct_prob * prob, axis=0, keepdims=True))
    ct_score = ct_score.astype(BF)
    ct_query = join_heads(mm_tn(ct_score, keys), 8).astype(BF).astype(F32)
    ct_key = mm(ct_score, query_heads).astype(BF).astype(F32)
    ct_value = mm(prob_half, ct_heads).astype(BF)
    ct_triple = jnp.concatenate(
        [
            unit_back(query_raw, ct_query * lanes, block).astype(BF),
            unit_back(key_raw, ct_key, block).astype(BF),
            ct_value,
        ],
        axis=1,
    )
    ct_normed = mm_nt(ct_triple, attend[...]).astype(BF).astype(F32)
    ct_merged = target.astype(F32) + rms_back(merged, gain[...], ct_normed)
    back_out[...] = lanes_to_rows(ct_merged.astype(BF))


def fine_backward(
    back,
    grad_three,
    normed,
    raw_query,
    raw_key,
    query,
    normed_beside,
    raw_beside,
    keys,
    value,
    prob,
    attn,
    scale,
    output,
    merge,
    grad_out,
    above_out,
    below_out,
    mixed_out,
    ct_query_out,
    ct_key_out,
    ct_value_out,
    pieces_left,
    pieces_right,
):
    block = head_block()
    ct_merged = rows_to_lanes(back[...], 4)
    groups = [
        mm_nt(ct_merged, merge[256 * group : 256 * group + 256]).astype(BF) for group in range(4)
    ]
    ct_mixed = mm_tn(merge_order(), jnp.concatenate(groups, axis=0)).astype(BF)
    mixed_out[...] = ct_mixed
    ct_attn = mm_nt(ct_mixed, output[...]).astype(BF)
    ct_queries, ct_keys, ct_values = [], [], []
    for tile in range(2):
        at = 128 * tile
        ct_heads = split_heads(ct_attn[at : at + 128], 4)
        query_heads = split_heads(query[at : at + 128], 4)
        prob_half = prob[tile]
        wide = prob_half.astype(F32)
        ct_prob = mm_nt(value[at : at + 256], ct_heads)
        ct_score = wide * (ct_prob - jnp.sum(ct_prob * wide, axis=0, keepdims=True))
        ct_score = ct_score.astype(BF)
        ct_queries.append(join_heads(mm_tn(ct_score, keys[at : at + 256]), 4))
        ct_keys.append(mm(ct_score, query_heads))
        ct_values.append(mm(prob_half, ct_heads))
    both = []
    for at, parts, out in ((0, ct_keys, ct_key_out), (256, ct_values, ct_value_out)):
        first, second = parts
        middle = first[128:] + second[:128]
        own = jnp.concatenate([first[HALO:128], middle, second[128 : 128 + HALO]], axis=0)
        upper, lower = first[:HALO], second[128 + HALO : 128 + 2 * HALO]
        out[...] = own.astype(BF)
        above_out[:, at : at + 256] = upper.astype(BF)
        below_out[:, at : at + 256] = lower.astype(BF)
        both.append(jnp.concatenate([own, upper, lower], axis=0))
    ct_query = jnp.concatenate(ct_queries, axis=0) * scale_lanes(scale, 4)
    ct_query = unit_back(raw_query[...].astype(F32), ct_query, block).astype(BF)
    ct_query_out[...] = ct_query
    raw_keys = jnp.concatenate([raw_key[...], raw_beside[...]], axis=0).astype(F32)
    ct_key = unit_back(raw_keys, both[0], block).astype(BF)
    normed_all = jnp.concatenate([normed[...], normed_beside[...]], axis=0)
    grads = [
        mm_tn(normed[...], ct_query),
        mm_tn(normed_all, ct_key),
        mm_tn(normed_all, both[1].astype(BF)),
    ]
    last = mm_tn(attn[...], ct_mixed)
    for half, pieces in enumerate((pieces_left, pieces_right)):
        lanes = slice(128 * half, 128 * half + 128)
        for at, grad in enumerate(grads):
            pieces[pl.ds(at, 256, stride=3), :] = grad[:, lanes]
        pieces[768:] = last[:, lanes]
        for row in range(8):
            for quarter in range(4):
                part = pieces[pl.ds(4 * row + quarter, 32, stride=32), :].astype(BF)
                at = 256 * quarter + 128 * half
                grad_out[64 * row : 64 * row + 32, at : at + 128] = part
    for row in range(8):
        grad_out[64 * row + 32 : 64 * row + 64, :] = grad_three[32 * row : 32 * row + 32]


def fine_finish(
    from_above,
    from_below,
    ct_query,
    ct_key,
    ct_value,
    raw_key,
    ct_mixed,
    tokens,
    gain,
    attend,
    tokens_out,
    done_out,
):
    above, below = from_above[...].astype(F32), from_below[...].astype(F32)

    def with_edges(own, at):
        return jnp.concatenate(
            [
                own[:HALO].astype(F32) + above[:, at : at + 256],
                own[HALO : 256 - HALO].astype(F32),
                own[256 - HALO :].astype(F32) + below[:, at : at + 256],
            ],
            axis=0,
        ).astype(BF)

    key_total = with_edges(ct_key[...], 0).astype(F32)
    value_total = with_edges(ct_value[...], 256)
    ct_key_raw = unit_back(raw_key[...].astype(F32), key_total, head_block()).astype(BF)
    ct_triple = jnp.concatenate([ct_query[...], ct_key_raw, value_total], axis=1)
    ct_normed = mm_nt(ct_triple, attend[...]).astype(BF).astype(F32)
    own = tokens[...].astype(F32)
    total = ct_mixed[...].astype(F32) + rms_back(own, gain[...], ct_normed)
    tokens_out[...] = total.astype(BF)
    done_out[...] = jnp.zeros((8, 128), F32)


def add_rows(shares, out):
    total = shares[0].astype(F32)
    for row in range(1, 8):
        total += shares[row].astype(F32)
    out[...] = lanes_to_rows(total.astype(BF))


def add_frames(shares, done, out):
    del done
    total = shares[0].astype(F32)
    for frame in range(1, 64):
        total += shares[frame].astype(F32)
    out[...] = total


class Late:
    def __init__(self, copy, ref):
        self.copy, self.ref = copy, ref

    def wait(self):
        if self.copy is not None:
            self.copy.wait()
            self.copy = None

    def __getitem__(self, index):
        self.wait()
        return self.ref[index]


def split(values, *sizes):
    out, at = [], 0
    for size in sizes:
        out.append(values[at : at + size])
        at += size
    return out


def near(shape, dtype=BF):
    return pltpu.VMEM(shape, dtype)


def call(kernel, outs, *args, smem=0, scratch=(), cost=None):
    local = pl.BlockSpec(memory_space=pltpu.VMEM)
    scalar = pl.BlockSpec(memory_space=pltpu.SMEM)
    return pl.pallas_call(
        kernel,
        out_shape=outs,
        in_specs=[scalar] * smem + [local] * (len(args) - smem),
        scratch_shapes=scratch,
        out_specs=[local] * len(outs),
        compiler_params=pltpu.CompilerParams(vmem_limit_bytes=VMEM_BYTES),
        cost_estimate=cost,
    )(*args)


def fetch_and_call(kernel, outs, used, *args, cost=None):
    count = len(args)
    local = pl.BlockSpec(memory_space=pltpu.VMEM)
    hbm = pl.BlockSpec(memory_space=pltpu.HBM)

    def run(*refs):
        sources, held, rest = refs[:count], refs[count : 2 * count], refs[2 * count :]
        sems = rest[-1]
        late = []
        for at in range(count):
            copy = pltpu.make_async_copy(sources[at], held[at], sems.at[at])
            copy.start()
            late.append(Late(copy, held[at]))
        kernel(*late[:used], *rest[:-1])
        for one in late:
            one.wait()

    return pl.pallas_call(
        run,
        out_shape=[near(arg.shape, arg.dtype) for arg in args] + outs,
        in_specs=[hbm] * count,
        out_specs=[local] * (count + len(outs)),
        scratch_shapes=[pltpu.SemaphoreType.DMA((count,))],
        compiler_params=pltpu.CompilerParams(vmem_limit_bytes=VMEM_BYTES),
        cost_estimate=cost,
    )(*[pltpu.with_memory_space_constraint(arg, pltpu.HBM) for arg in args])


def body(
    tokens,
    keep_mask,
    gain_two,
    attend_two,
    scale_two,
    output_two,
    merge_weight,
    gain_three,
    attend_three,
    scale_three,
    output_three,
    cotangent,
):
    count = lax.axis_size("rows")
    to_next = [(i, i + 1) for i in range(count - 1)]
    to_last = [(i + 1, i) for i in range(count - 1)]
    own = tokens.reshape(256, 256)
    above = lax.ppermute(own[256 - HALO :], "rows", to_next)
    below = lax.ppermute(own[:HALO], "rows", to_last)
    rank = lax.axis_index("rows").astype(jnp.int32).reshape(1)
    square = (256, 256)
    (
        (own, gain_two, attend_two, scale_two, keep, output_two, cot, merge_weight),
        (gain_three, attend_three, scale_three, output_three),
        (normed, raw_query, raw_key, query, own_keys, own_value),
    ) = split(
        fetch_and_call(
            fine_project,
            [near(square)] * 6,
            4,
            own,
            gain_two.reshape(1, 256),
            attend_two,
            scale_two.reshape(1, 4),
            keep_mask.reshape(128, 16).T,
            output_two,
            cotangent.reshape(64, 512),
            merge_weight,
            gain_three.reshape(1, 512),
            attend_three,
            scale_three.reshape(1, 8),
            output_three,
            cost=pl.CostEstimate(flops=170_000_000, bytes_accessed=5_000_000, transcendentals=0),
        ),
        8,
        4,
        6,
    )
    normed_beside, raw_beside, keys, value, prob, attn, place = call(
        fine_forward,
        [
            near((96, 256)),
            near((96, 256)),
            near((384, 256)),
            near((384, 256)),
            near((2, 256, 512)),
            near(square),
            jax.ShapeDtypeStruct((512, 128), BF),
        ],
        rank,
        above,
        below,
        query,
        own_keys,
        own_value,
        own,
        gain_two,
        attend_two,
        keep,
        output_two,
        cot,
        merge_weight,
        smem=1,
    )
    place = lax.all_to_all(place.reshape(64, 8, 128), "frames", 0, 0, tiled=True)
    grad_three, back = call(
        coarse,
        [near((256, 1024)), jax.ShapeDtypeStruct((256, 128), BF)],
        place.reshape(512, 128),
        gain_three,
        attend_three,
        scale_three,
        output_three,
    )
    back = lax.all_to_all(back.reshape(64, 4, 128), "frames", 0, 0, tiled=True)
    grads, up, down, ct_mixed, ct_query, ct_key, ct_value = call(
        fine_backward,
        [
            jax.ShapeDtypeStruct((512, 1024), BF),
            jax.ShapeDtypeStruct((HALO, 512), BF),
            jax.ShapeDtypeStruct((HALO, 512), BF),
            near(square),
            near(square),
            near(square),
            near(square),
        ],
        back.reshape(256, 128),
        grad_three,
        normed,
        raw_query,
        raw_key,
        query,
        normed_beside,
        raw_beside,
        keys,
        value,
        prob,
        attn,
        scale_two,
        output_two,
        merge_weight,
        scratch=[pltpu.VMEM((1024, 128), F32)] * 2,
    )
    from_below = lax.ppermute(up, "rows", to_last)
    from_above = lax.ppermute(down, "rows", to_next)
    tokens_grad, done = call(
        fine_finish,
        [jax.ShapeDtypeStruct(square, BF), near((8, 128), F32)],
        from_above,
        from_below,
        ct_query,
        ct_key,
        ct_value,
        raw_key,
        ct_mixed,
        own,
        gain_two,
        attend_two,
        cost=pl.CostEstimate(flops=170_000_000, bytes_accessed=2_000_000, transcendentals=0),
    )
    shares = lax.all_to_all(grads.reshape(count, 64, 1024), "rows", 0, 0, tiled=True)
    (shares,) = call(add_rows, [jax.ShapeDtypeStruct((512, 128), BF)], shares)
    shares = lax.all_to_all(shares.reshape(64, 8, 128), "frames", 0, 0, tiled=True)
    (total,) = call(add_frames, [jax.ShapeDtypeStruct((8, 128), F32)], shares, done)
    return (tokens_grad.reshape(tokens.shape), total.reshape(1, 1024))


def solution(mesh):
    return jax.shard_map(
        body,
        mesh=mesh,
        in_specs=(
            P("frames", "rows", None, None),
            P("frames", None, None),
            P(),
            P(),
            P(),
            P(),
            P(),
            P(),
            P(),
            P(),
            P(),
            P("frames", "rows", None, None),
        ),
        out_specs=(P("frames", "rows", None, None), P(("frames", "rows"), None)),
        check_vma=False,
    )
```

time: 536 us -> 106 us (0.20)
  waiting for transfers between devices: 296 us -> 8.61 us
  local copies, waits for them, and re-layouts: 103 us -> 0.76 us
  blocking collectives: 0 us -> 66.8 us
  other arithmetic: 43.1 us -> 0 us
  starting transfers between devices: 54.4 us -> 14.9 us
  matrix products: 20.6 us -> 0 us
  between operations: 15.4 us -> 0.72 us
  Pallas kernels: 0 us -> 14.1 us
    unnamed x2 -> x0, waiting for transfers between devices: 273 us -> none
    all_to_all x0 -> x3, blocking collectives: none -> 66.8 us  [the longest x1 29.9 us: body(): lax.all_to_all(place.reshape(64, 8, 128), 'frames', 0, 0, tiled=True)]
    all_to_all x4 -> x1, starting transfers between devices: 42.2 us -> 5.86 us  [body(): lax.all_to_all(shares.reshape(64, 8, 128), 'frames', 0, 0, tiled=True)]
    unnamed x151 -> x0, local copies, waits for them, and re-layouts: 30.8 us -> none
    reshape x15 -> x0, local copies, waits for them, and re-layouts: 22 us -> none  [the longest x2 8.82 us: neighbour_attention(): windows.reshape(frames, row_tiles, col_tiles, 196, 2, heads, head)]
    dot_general x24 -> x0, matrix products: 20.6 us -> none  [the longest x12 8.6 us: float_dot(): jnp.dot(left, right, preferred_element_type=jnp.float32, precision=lax.Pr...]
    all_to_all x4 -> x1, waiting for transfers between devices: 23.5 us -> 3.84 us  [body(): lax.all_to_all(shares.reshape(64, 8, 128), 'frames', 0, 0, tiled=True)]
    pallas_call x0 -> x7, Pallas kernels: none -> 14.1 us  [the longest x6 11.8 us: call(): pl.pallas_call(kernel, out_shape=outs, in_specs=[scalar] * smem + [local]...]
  transfers between devices with their start and end apart: 9 -> 5, of which waited for: 4 -> 3; matrix products, arithmetic and copies ran while one was open for 12% -> 0% of each run, Pallas kernels for 0% -> 3%
where the time goes in v1:
time: 106 us
  blocking collectives  66.8 us (63%)
  starting transfers between devices  14.9 us (14%)
  Pallas kernels  14.1 us (13%)
  waiting for transfers between devices  8.61 us (8%)
    all_to_all x1, blocking collectives, body(): lax.all_to_all(place.reshape(64, 8, 128), 'frames', 0, 0, tiled=True)  29.9 us
    all_to_all x1, blocking collectives, body(): lax.all_to_all(grads.reshape(count, 64, 1024), 'rows', 0, 0, tiled=True)  20.6 us
    all_to_all x1, blocking collectives, body(): back = lax.all_to_all(back.reshape(64, 4, 128), 'frames', 0, 0, tiled=True)  16.3 us
    pallas_call x6, Pallas kernels, call(): pl.pallas_call(kernel, out_shape=outs, in_specs=[scalar] * smem + [local]...  11.8 us
    all_to_all x1, starting transfers between devices, body(): lax.all_to_all(shares.reshape(64, 8, 128), 'frames', 0, 0, tiled=True)  5.86 us
    ppermute x1, starting transfers between devices, body(): above = lax.ppermute(own[256 - HALO:], 'rows', to_next)  4.02 us
    all_to_all x1, waiting for transfers between devices, body(): lax.all_to_all(shares.reshape(64, 8, 128), 'frames', 0, 0, tiled=True)  3.84 us
    ppermute x1, waiting for transfers between devices, body(): from_below = lax.ppermute(up, 'rows', to_last)  3.82 us
  transfers between devices with their start and end apart: 5, of which 3 were waited for; matrix products, arithmetic and copies ran while one was open for 0% of the time, Pallas kernels for 3%

profile of v1, /device:TPU:1, one launch (start us, length us, event | category | flops | bytes accessed | tf_op | source)
XLA Modules:
  0.0 105.9 jit_solution(888592779540509507)
XLA Ops:
  0.6 0.8 fusion
  1.4 4.0 %collective-permute-start = (bf16[48,256]{1,0:T(8,128)(2,1)S(1)}, bf16[48,256]{1,0:T(8,128)(2,1)S(1)}, u32[]{:S(2)}, u32[]{:S(2)}) collective-permute-start(bf16[48,256]{1,0:T(8,128)(2,1)S(1)} %bitcast.28), channel_id=1, source_target_pairs={{0,1},{1,2},{2,3},{3,4},{4,5},{5,6},{6,7},{8,9},{9,10},{10,11},{11... | collective-permute-start | bytes 73736 | tf_op jit(solution)/shard_map/ppermute | solution.py:469
  5.4 1.3 %collective-permute-start.1 = (bf16[48,256]{1,0:T(8,128)(2,1)S(1)}, bf16[48,256]{1,0:T(8,128)(2,1)S(1)}, u32[]{:S(2)}, u32[]{:S(2)}) collective-permute-start(bf16[48,256]{1,0:T(8,128)(2,1)S(1)} %bitcast.27), channel_id=1, source_target_pairs={{1,0},{2,1},{3,2},{4,3},{5,4},{6,5},{7,6},{9,8},{10,9},{11,10},{12... | collective-permute-start | bytes 73736 | tf_op jit(solution)/shard_map/ppermute | solution.py:470
  6.7 2.3 %shard_map.131 = (bf16[256,256]{1,0:T(8,128)(2,1)S(1)}, f32[1,256]{1,0:T(1,128)S(1)}, bf16[256,768]{1,0:T(8,128)(2,1)S(1)}, f32[1,4]{1,0:T(1,128)S(1)}, s32[16,1...) custom-call(bf16[256,256]{1,0:T(8,128)(2,1)} %bitcast.25, ...), custom_call_target="tpu_custom_call" | custom-call | flops 170000000 | bytes 5000000 | tf_op jit(solution)/shard_map/pallas_call | solution.py:440
  9.0 0.0 collective-permute-done.above
  9.0 0.9 collective-permute-done.1.below
  10.0 2.2 %shard_map.132 = (bf16[96,256]{1,0:T(8,128)(2,1)S(1)}, bf16[96,256]{1,0:T(8,128)(2,1)S(1)}, bf16[384,256]{1,0:T(8,128)(2,1)S(1)}, bf16[384,256]{1,0:T(8,128)(2,1...) custom-call(s32[1]{0:T(128)} %bitcast.rank, ...), custom_call_target="tpu_custom_call" | custom-call | tf_op jit(solution)/shard_map/pallas_call | solution.py:412
  12.2 29.9 %all_to_all.20 = bf16[64,8,128]{2,1,0:T(8,128)(2,1)S(1)} all-to-all(bf16[64,8,128]{2,1,0:T(8,128)(2,1)S(1)} %bitcast.23), channel_id=1, replica_groups=mesh['frames'=64,'rows'=8] {'frames'}, dimensions={0} | all-to-all | bytes 262144 | tf_op jit(solution)/shard_map/all_to_all | solution.py:526
  42.2 3.7 %shard_map.133 = (bf16[256,1024]{1,0:T(8,128)(2,1)S(1)}, bf16[256,128]{1,0:T(8,128)(2,1)S(1)}) custom-call(bf16[512,128]{1,0:T(8,128)(2,1)S(1)} %bitcast.21, f32[1,512]{1,0:T(1,128)S(1)} %get-tuple-element.49.gain, bf16[512,1536]{1,0:T(8,128)(2,1)S(1)} %get-tuple-element.50.attend, f32[1,8]{1,0:T(1,128)S(1)} %get-tuple-element.51.scale, ...), custom_call_target="tpu_custom_call" | custom-call | tf_op jit(solution)/shard_map/pallas_call | solution.py:412
  45.9 16.3 %all_to_all.21 = bf16[64,4,128]{2,1,0:T(4,128)(2,1)S(1)} all-to-all(bf16[64,4,128]{2,1,0:T(4,128)(2,1)S(1)} %bitcast.24), channel_id=1, replica_groups=mesh['frames'=64,'rows'=8] {'frames'}, dimensions={0} | all-to-all | bytes 131072 | tf_op jit(solution)/shard_map/all_to_all | solution.py:536
  62.1 3.0 %shard_map.134 = (bf16[512,1024]{1,0:T(8,128)(2,1)S(1)}, bf16[48,512]{1,0:T(8,128)(2,1)S(1)}, bf16[48,512]{1,0:T(8,128)(2,1)S(1)}, bf16[256,256]{1,0:T(8,128)(2,...) custom-call(bf16[256,128]{1,0:T(8,128)(2,1)S(1)} %bitcast.22, ...), custom_call_target="tpu_custom_call" | custom-call | tf_op jit(solution)/shard_map/pallas_call | solution.py:412
  65.1 20.6 %all_to_all.22.shares = bf16[8,64,1024]{2,1,0:T(8,128)(2,1)S(1)} all-to-all(bf16[8,64,1024]{2,1,0:T(8,128)(2,1)S(1)} %bitcast.20), channel_id=1, replica_groups=mesh['frames'=64,'rows'=8] {'rows'}, dimensions={0} | all-to-all | bytes 2097152 | tf_op jit(solution)/shard_map/all_to_all | solution.py:582
  85.7 1.0 shard_map.136
  86.8 5.9 %all-to-all-start.3 = ((bf16[64,8,128]{2,1,0:T(8,128)(2,1)}), bf16[64,8,128]{2,1,0:T(8,128)(2,1)S(1)}, u32[]{:S(2)}, u32[]{:S(2)}) async-start(bf16[64,8,128]{2,1,0:T(8,128)(2,1)} %bitcast.17), calls=%async_computation.3 | async-start | bytes 262144 | tf_op jit(solution)/shard_map/all_to_all | solution.py:584
  92.6 2.5 %collective-permute-start.2 = (bf16[48,512]{1,0:T(8,128)(2,1)S(1)}, bf16[48,512]{1,0:T(8,128)(2,1)S(1)}, u32[]{:S(2)}, u32[]{:S(2)}) collective-permute-start(bf16[48,512]{1,0:T(8,128)(2,1)S(1)} %get-tuple-element.65), channel_id=1, source_target_pairs={{0,1},{1,2},{2,3},{3,4},{4,5},{5,6},{6,7},{8,9},{9,10},{10,11},{11... | collective-permute-start | bytes 147464 | tf_op jit(solution)/shard_map/ppermute | solution.py:566
  95.1 1.3 %collective-permute-start.3 = (bf16[48,512]{1,0:T(8,128)(2,1)S(1)}, bf16[48,512]{1,0:T(8,128)(2,1)S(1)}, u32[]{:S(2)}, u32[]{:S(2)}) collective-permute-start(bf16[48,512]{1,0:T(8,128)(2,1)S(1)} %get-tuple-element.66), channel_id=1, source_target_pairs={{1,0},{2,1},{3,2},{4,3},{5,4},{6,5},{7,6},{9,8},{10,9},{11,10},{12... | collective-permute-start | bytes 147464 | tf_op jit(solution)/shard_map/ppermute | solution.py:565
  96.4 0.0 collective-permute-done.2.from_above
  96.4 3.8 %collective-permute-done.3.from_below = bf16[48,512]{1,0:T(8,128)(2,1)S(1)} collective-permute-done((bf16[48,512]{1,0:T(8,128)(2,1)S(1)}, bf16[48,512]{1,0:T(8,128)(2,1)S(1)}, u32[]{:S(2)}, u32[]{:S(2)}) %collective-permute-start.3) | collective-permute-done | bytes 49184 | tf_op jit(solution)/shard_map/ppermute | solution.py:565
  100.3 1.2 %shard_map.135 = (bf16[256,256]{1,0:T(8,128)(2,1)}, f32[8,128]{1,0:T(8,128)S(1)}) custom-call(bf16[48,512]{1,0:T(8,128)(2,1)S(1)} %collective-permute-done.2.from_above, bf16[48,512]{1,0:T(8,128)(2,1)S(1)} %collective-permute-done.3.from_below, bf16[256,256]{1,0:T(8,128)(2,1)S(1)} %get-tuple-element.67.ct_query, ...), custom_call_target="tpu_custom_call" | custom-call | flops 170000000 | bytes 2000000 | tf_op jit(solution)/shard_map/pallas_call | solution.py:412
  101.4 3.8 %all-to-all-done.3.shares = bf16[64,8,128]{2,1,0:T(8,128)(2,1)S(1)} async-done(((bf16[64,8,128]{2,1,0:T(8,128)(2,1)}), bf16[64,8,128]{2,1,0:T(8,128)(2,1)S(1)}, u32[]{:S(2)}, u32[]{:S(2)}) %all-to-all-start.3) | async-done | bytes 131104 | tf_op jit(solution)/shard_map/all_to_all | solution.py:584
  105.3 0.7 shard_map.137
Async XLA Ops:
  1.4 7.6 %collective-permute-start = (bf16[48,256]{1,0:T(8,128)(2,1)S(1)}, bf16[48,256]{1,0:T(8,128)(2,1)S(1)}, u32[]{:S(2)}, u32[]{:S(2)}) collective-permute-start(bf16[48,256]{1,0:T(8,128)(2,1)S(1)} %bitcast.28), channel_id=1, source_target_pairs={{0,1},{1,2},{2,3},{3,4},{4,5},{5,6},{6,7},{8,9},{9,10},{10,11},{11... | collective-permute-start | bytes 73736 | tf_op jit(solution)/shard_map/ppermute | solution.py:469
  5.4 4.6 %collective-permute-start.1 = (bf16[48,256]{1,0:T(8,128)(2,1)S(1)}, bf16[48,256]{1,0:T(8,128)(2,1)S(1)}, u32[]{:S(2)}, u32[]{:S(2)}) collective-permute-start(bf16[48,256]{1,0:T(8,128)(2,1)S(1)} %bitcast.27), channel_id=1, source_target_pairs={{1,0},{2,1},{3,2},{4,3},{5,4},{6,5},{7,6},{9,8},{10,9},{11,10},{12... | collective-permute-start | bytes 73736 | tf_op jit(solution)/shard_map/ppermute | solution.py:470
  86.8 18.5 %all-to-all-start.3 = ((bf16[64,8,128]{2,1,0:T(8,128)(2,1)}), bf16[64,8,128]{2,1,0:T(8,128)(2,1)S(1)}, u32[]{:S(2)}, u32[]{:S(2)}) async-start(bf16[64,8,128]{2,1,0:T(8,128)(2,1)} %bitcast.17), calls=%async_computation.3 | async-start | bytes 262144 | tf_op jit(solution)/shard_map/all_to_all | solution.py:584
  92.6 3.8 %collective-permute-start.2 = (bf16[48,512]{1,0:T(8,128)(2,1)S(1)}, bf16[48,512]{1,0:T(8,128)(2,1)S(1)}, u32[]{:S(2)}, u32[]{:S(2)}) collective-permute-start(bf16[48,512]{1,0:T(8,128)(2,1)S(1)} %get-tuple-element.65), channel_id=1, source_target_pairs={{0,1},{1,2},{2,3},{3,4},{4,5},{5,6},{6,7},{8,9},{9,10},{10,11},{11... | collective-permute-start | bytes 147464 | tf_op jit(solution)/shard_map/ppermute | solution.py:566
  95.1 5.1 %collective-permute-start.3 = (bf16[48,512]{1,0:T(8,128)(2,1)S(1)}, bf16[48,512]{1,0:T(8,128)(2,1)S(1)}, u32[]{:S(2)}, u32[]{:S(2)}) collective-permute-start(bf16[48,512]{1,0:T(8,128)(2,1)S(1)} %get-tuple-element.66), channel_id=1, source_target_pairs={{1,0},{2,1},{3,2},{4,3},{5,4},{6,5},{7,6},{9,8},{10,9},{11,10},{12... | collective-permute-start | bytes 147464 | tf_op jit(solution)/shard_map/ppermute | solution.py:565

commit v2 on v1

--- a/solution.py
+++ b/solution.py
@@ -87,35 +87,44 @@
     return scale * ct - values * (scale * scale * scale * head_sum(ct * values, block))
 
 
-def ordering(size, target):
-    return zero_one(iota((size, target.shape[1]), 0) == target)
-
-
-def merge_order():
-    patch = iota((1, 256), 1)
-    group = ((patch >> 3) & 2) + (patch & 1)
-    return ordering(256, (group << 6) + ((patch >> 5) << 3) + ((patch >> 1) & 7))
-
-
-def bits(count):
-    return count.bit_length() - 1
-
-
-def lanes_to_rows(values):
+def lanes_to_rows(values, rows, base):
     count, blocks = values.shape[0], values.shape[1] // 128
-    stacked = jnp.concatenate([values[:, 128 * j : 128 * j + 128] for j in range(blocks)], axis=0)
-    at = iota((1, count * blocks), 1)
-    target = ((at & (count - 1)) << bits(blocks)) + (at >> bits(count))
-    return mm(ordering(count * blocks, target), stacked).astype(BF)
-
-
-def rows_to_lanes(values, blocks):
-    total = values.shape[0]
-    count = total // blocks
-    at = iota((1, total), 1)
-    target = ((at & (blocks - 1)) << bits(count)) + (at >> bits(blocks))
-    stacked = mm(ordering(total, target), values).astype(BF)
-    return jnp.concatenate([stacked[count * j : count * j + count] for j in range(blocks)], axis=1)
+    for j in range(blocks):
+        rows[pl.ds(base + j, count, stride=blocks), :] = values[:, 128 * j : 128 * j + 128]
+
+
+def rows_to_lanes(rows, base, count, blocks):
+    parts = [rows[pl.ds(base + j, count, stride=blocks), :] for j in range(blocks)]
+    return jnp.concatenate(parts, axis=1)
+
+
+def merged_spots():
+    return [[32 * a + 16 * (group >> 1) + (group & 1) for a in range(8)] for group in range(4)]
+
+
+def split_patches(mixed, rows, base):
+    for half in range(2):
+        at = base + 256 * half
+        rows[at : at + 256] = mixed[:, 128 * half : 128 * half + 128]
+    groups = []
+    for spots in merged_spots():
+        halves = [
+            jnp.concatenate(
+                [rows[pl.ds(base + 256 * half + spot, 8, stride=2), :] for spot in spots], axis=0
+            )
+            for half in range(2)
+        ]
+        groups.append(jnp.concatenate(halves, axis=1).astype(BF))
+    return groups
+
+
+def join_patches(groups, rows, base):
+    for spots, group in zip(merged_spots(), groups):
+        for a, spot in enumerate(spots):
+            for half in range(2):
+                part = group[8 * a : 8 * a + 8, 128 * half : 128 * half + 128]
+                rows[pl.ds(base + 256 * half + spot, 8, stride=2), :] = part
+    return jnp.concatenate([rows[base : base + 256], rows[base + 256 : base + 512]], axis=1)
 
 
 def fine_project(
@@ -149,6 +158,7 @@
 
 def fine_forward(
     rank,
+    core,
     above,
     below,
     query,
@@ -161,14 +171,30 @@
     output,
     cotangent,
     merge,
+    gain_far,
+    attend_far,
+    scale_far,
+    output_far,
     beside_out,
     raw_out,
     key_out,
     value_out,
     prob_out,
     attn_out,
+    gain_out,
+    attend_out,
+    scale_out,
+    output_out,
     place_out,
+    rows,
+    sems,
 ):
+    far = (gain_far, attend_far, scale_far, output_far)
+    close = (gain_out, attend_out, scale_out, output_out)
+    copies = [pltpu.make_async_copy(far[at], close[at], sems.at[at]) for at in range(4)]
+    for copy in copies:
+        copy.start()
+    del core
     halo = jnp.concatenate([above[...], below[...]], axis=0).astype(F32)
     normed = rms(halo, gain[...])
     beside_out[...] = normed
@@ -196,17 +222,20 @@
     attn = jnp.concatenate(parts, axis=0).astype(BF)
     attn_out[...] = attn
     mixed = (tokens[...].astype(F32) + mm(attn, output[...])).astype(BF)
-    patches = mm(merge_order(), mixed).astype(BF)
-    merged = mm(patches[:64], merge[:256])
+    patches = split_patches(mixed.astype(F32), rows, 0)
+    merged = mm(patches[0], merge[:256])
     for group in range(1, 4):
-        merged += mm(patches[64 * group : 64 * group + 64], merge[256 * group : 256 * group + 256])
-    both = jnp.concatenate([merged.astype(BF), cotangent[...]], axis=1)
-    place_out[...] = lanes_to_rows(both)
-
-
-def coarse(place, gain, attend, scale, output, grad_out, back_out):
-    both = rows_to_lanes(place[...], 8)
-    merged, target = both[:, :512].astype(F32), both[:, 512:]
+        merged += mm(patches[group], merge[256 * group : 256 * group + 256])
+    lanes_to_rows(jnp.concatenate([merged, cotangent[...].astype(F32)], axis=1), rows, 512)
+    place_out[...] = rows[512:].astype(BF)
+    for copy in copies:
+        copy.wait()
+
+
+def coarse(place, gain, attend, scale, output, grad_out, back_out, rows, back_rows):
+    rows[:512] = place[...].astype(F32)
+    both = rows_to_lanes(rows, 0, 64, 8)
+    merged, target = both[:, :512], both[:, 512:].astype(BF)
     block = head_block()
     lanes = scale_lanes(scale, 8)
     normed = rms(merged, gain[...])
@@ -220,10 +249,10 @@
     prob = weight / jnp.sum(weight, axis=0, keepdims=True)
     prob_half = prob.astype(BF)
     attn = join_heads(mm_tn(prob_half, value), 8).astype(BF)
-    at = iota((1, 512), 1)
-    slot = ((at & 1) << 8) + (((at >> 1) & 7) << 5) + (at >> 4)
-    grad = mm_tn(mm_nt(attn, ordering(512, slot)).astype(BF), target).astype(BF)
-    grad_out[...] = jnp.concatenate([grad[:256], grad[256:]], axis=1)
+    grad = mm_tn(attn, target)
+    for part in range(4):
+        rows[pl.ds(part, 512, stride=4), :] = grad[:, 128 * part : 128 * part + 128]
+    grad_out[...] = rows[...].astype(BF)
     ct_attn = mm_nt(target, output[...]).astype(BF)
     ct_heads = split_heads(ct_attn, 8)
     ct_prob = mm_nt(value, ct_heads)
@@ -242,10 +271,12 @@
     )
     ct_normed = mm_nt(ct_triple, attend[...]).astype(BF).astype(F32)
     ct_merged = target.astype(F32) + rms_back(merged, gain[...], ct_normed)
-    back_out[...] = lanes_to_rows(ct_merged.astype(BF))
+    lanes_to_rows(ct_merged, back_rows, 0)
+    back_out[...] = back_rows[...].astype(BF)
 
 
 def fine_backward(
+    core,
     back,
     grad_three,
     normed,
@@ -261,22 +292,21 @@
     scale,
     output,
     merge,
-    grad_out,
+    keep_out,
+    send_out,
     above_out,
     below_out,
     mixed_out,
     ct_query_out,
     ct_key_out,
     ct_value_out,
-    pieces_left,
-    pieces_right,
+    rows,
 ):
     block = head_block()
-    ct_merged = rows_to_lanes(back[...], 4)
-    groups = [
-        mm_nt(ct_merged, merge[256 * group : 256 * group + 256]).astype(BF) for group in range(4)
-    ]
-    ct_mixed = mm_tn(merge_order(), jnp.concatenate(groups, axis=0)).astype(BF)
+    rows[:256] = back[...].astype(F32)
+    ct_merged = rows_to_lanes(rows, 0, 64, 4).astype(BF)
+    groups = [mm_nt(ct_merged, merge[256 * group : 256 * group + 256]) for group in range(4)]
+    ct_mixed = join_patches(groups, rows, 256).astype(BF)
     mixed_out[...] = ct_mixed
     ct_attn = mm_nt(ct_mixed, output[...]).astype(BF)
     ct_queries, ct_keys, ct_values = [], [], []
@@ -314,18 +344,23 @@
         mm_tn(normed_all, both[1].astype(BF)),
     ]
     last = mm_tn(attn[...], ct_mixed)
-    for half, pieces in enumerate((pieces_left, pieces_right)):
+    for half in range(2):
         lanes = slice(128 * half, 128 * half + 128)
         for at, grad in enumerate(grads):
-            pieces[pl.ds(at, 256, stride=3), :] = grad[:, lanes]
-        pieces[768:] = last[:, lanes]
-        for row in range(8):
-            for quarter in range(4):
-                part = pieces[pl.ds(4 * row + quarter, 32, stride=32), :].astype(BF)
-                at = 256 * quarter + 128 * half
-                grad_out[64 * row : 64 * row + 32, at : at + 128] = part
-    for row in range(8):
-        grad_out[64 * row + 32 : 64 * row + 64, :] = grad_three[32 * row : 32 * row + 32]
+            rows[pl.ds(2 * at + half, 256, stride=6), :] = grad[:, lanes]
+        rows[pl.ds(1536 + half, 256, stride=2), :] = last[:, lanes]
+    own_even = core[0] == 0
+    for pair in range(16):
+        even = rows[128 * pair : 128 * pair + 64].astype(BF)
+        odd = rows[128 * pair + 64 : 128 * pair + 128].astype(BF)
+        at = 64 * pair
+        keep_out[at : at + 64] = jnp.where(own_even, even, odd)
+        send_out[at : at + 64] = jnp.where(own_even, odd, even)
+        even = grad_three[128 * pair : 128 * pair + 64]
+        odd = grad_three[128 * pair + 64 : 128 * pair + 128]
+        at = 1024 + 64 * pair
+        keep_out[at : at + 64] = jnp.where(own_even, even, odd)
+        send_out[at : at + 64] = jnp.where(own_even, odd, even)
 
 
 def fine_finish(
@@ -365,19 +400,16 @@
     done_out[...] = jnp.zeros((8, 128), F32)
 
 
-def add_rows(shares, out):
-    total = shares[0].astype(F32)
-    for row in range(1, 8):
-        total += shares[row].astype(F32)
-    out[...] = lanes_to_rows(total.astype(BF))
-
-
-def add_frames(shares, done, out):
+def add_pair(kept, sent, out):
+    out[...] = (kept[...].astype(F32) + sent[...].astype(F32)).astype(BF)
+
+
+def add_all(shares, done, out):
     del done
-    total = shares[0].astype(F32)
-    for frame in range(1, 64):
-        total += shares[frame].astype(F32)
-    out[...] = total
+    total = [shares[at].astype(F32) for at in range(4)]
+    for device in range(4, shares.shape[0]):
+        total[device % 4] += shares[device].astype(F32)
+    out[...] = (total[0] + total[1]) + (total[2] + total[3])
 
 
 class Late:
@@ -406,13 +438,18 @@
     return pltpu.VMEM(shape, dtype)
 
 
-def call(kernel, outs, *args, smem=0, scratch=(), cost=None):
+def call(kernel, outs, *args, smem=0, far=0, scratch=(), cost=None):
+    close = len(args) - far
+    args = list(args[:close]) + [
+        pltpu.with_memory_space_constraint(arg, pltpu.HBM) for arg in args[close:]
+    ]
     local = pl.BlockSpec(memory_space=pltpu.VMEM)
+    hbm = pl.BlockSpec(memory_space=pltpu.HBM)
     scalar = pl.BlockSpec(memory_space=pltpu.SMEM)
     return pl.pallas_call(
         kernel,
         out_shape=outs,
-        in_specs=[scalar] * smem + [local] * (len(args) - smem),
+        in_specs=[scalar] * smem + [local] * (close - smem) + [hbm] * far,
         scratch_shapes=scratch,
         out_specs=[local] * len(outs),
         compiler_params=pltpu.CompilerParams(vmem_limit_bytes=VMEM_BYTES),
@@ -469,10 +506,10 @@
     above = lax.ppermute(own[256 - HALO :], "rows", to_next)
     below = lax.ppermute(own[:HALO], "rows", to_last)
     rank = lax.axis_index("rows").astype(jnp.int32).reshape(1)
+    core = (lax.axis_index("frames") & 1).astype(jnp.int32).reshape(1)
     square = (256, 256)
     (
         (own, gain_two, attend_two, scale_two, keep, output_two, cot, merge_weight),
-        (gain_three, attend_three, scale_three, output_three),
         (normed, raw_query, raw_key, query, own_keys, own_value),
     ) = split(
         fetch_and_call(
@@ -487,17 +524,14 @@
             output_two,
             cotangent.reshape(64, 512),
             merge_weight,
-            gain_three.reshape(1, 512),
-            attend_three,
-            scale_three.reshape(1, 8),
-            output_three,
             cost=pl.CostEstimate(flops=170_000_000, bytes_accessed=5_000_000, transcendentals=0),
         ),
         8,
-        4,
         6,
     )
-    normed_beside, raw_beside, keys, value, prob, attn, place = call(
+    gain_three, scale_three = gain_three.reshape(1, 512), scale_three.reshape(1, 8)
+    three = (gain_three, attend_three, scale_three, output_three)
+    normed_beside, raw_beside, keys, value, prob, attn, *three, place = call(
         fine_forward,
         [
             near((96, 256)),
@@ -506,9 +540,11 @@
             near((384, 256)),
             near((2, 256, 512)),
             near(square),
+            *[near(weight.shape, weight.dtype) for weight in three],
             jax.ShapeDtypeStruct((512, 128), BF),
         ],
         rank,
+        core,
         above,
         below,
         query,
@@ -521,23 +557,25 @@
         output_two,
         cot,
         merge_weight,
-        smem=1,
+        *three,
+        smem=2,
+        far=4,
+        scratch=[pltpu.VMEM((1024, 128), F32), pltpu.SemaphoreType.DMA((4,))],
     )
     place = lax.all_to_all(place.reshape(64, 8, 128), "frames", 0, 0, tiled=True)
     grad_three, back = call(
         coarse,
-        [near((256, 1024)), jax.ShapeDtypeStruct((256, 128), BF)],
+        [near((2048, 128)), jax.ShapeDtypeStruct((256, 128), BF)],
         place.reshape(512, 128),
-        gain_three,
-        attend_three,
-        scale_three,
-        output_three,
+        *three,
+        scratch=[pltpu.VMEM((2048, 128), F32), pltpu.VMEM((256, 128), F32)],
     )
     back = lax.all_to_all(back.reshape(64, 4, 128), "frames", 0, 0, tiled=True)
-    grads, up, down, ct_mixed, ct_query, ct_key, ct_value = call(
+    kept, sent, up, down, ct_mixed, ct_query, ct_key, ct_value = call(
         fine_backward,
         [
-            jax.ShapeDtypeStruct((512, 1024), BF),
+            near((2048, 128)),
+            jax.ShapeDtypeStruct((2048, 128), BF),
             jax.ShapeDtypeStruct((HALO, 512), BF),
             jax.ShapeDtypeStruct((HALO, 512), BF),
             near(square),
@@ -545,6 +583,7 @@
             near(square),
             near(square),
         ],
+        core,
         back.reshape(256, 128),
         grad_three,
         normed,
@@ -560,8 +599,11 @@
         scale_two,
         output_two,
         merge_weight,
-        scratch=[pltpu.VMEM((1024, 128), F32)] * 2,
-    )
+        smem=1,
+        scratch=[pltpu.VMEM((2048, 128), F32)],
+    )
+    pairs = [(i, i ^ 1) for i in range(lax.axis_size("frames"))]
+    sent = lax.ppermute(sent, "frames", pairs)
     from_below = lax.ppermute(up, "rows", to_last)
     from_above = lax.ppermute(down, "rows", to_next)
     tokens_grad, done = call(
@@ -579,10 +621,18 @@
         attend_two,
         cost=pl.CostEstimate(flops=170_000_000, bytes_accessed=2_000_000, transcendentals=0),
     )
-    shares = lax.all_to_all(grads.reshape(count, 64, 1024), "rows", 0, 0, tiled=True)
-    (shares,) = call(add_rows, [jax.ShapeDtypeStruct((512, 128), BF)], shares)
-    shares = lax.all_to_all(shares.reshape(64, 8, 128), "frames", 0, 0, tiled=True)
-    (total,) = call(add_frames, [jax.ShapeDtypeStruct((8, 128), F32)], shares, done)
+    (shares,) = call(add_pair, [jax.ShapeDtypeStruct((2048, 128), BF)], kept, sent)
+    every = lax.axis_size("frames") * count
+    groups = [[at for at in range(every) if at // count % 2 == own] for own in (0, 1)]
+    shares = lax.all_to_all(
+        shares.reshape(every // 2, 8, 128),
+        ("frames", "rows"),
+        0,
+        0,
+        tiled=True,
+        axis_index_groups=groups,
+    )
+    (total,) = call(add_all, [jax.ShapeDtypeStruct((8, 128), F32)], shares, done)
     return (tokens_grad.reshape(tokens.shape), total.reshape(1, 1024))
 
 

time: 106 us -> 101 us (0.953); the launches traced: 106 us -> 99.8 us
  blocking collectives: 66.8 us -> 46.2 us
  waiting for transfers between devices: 8.61 us -> 17.7 us
  starting transfers between devices: 14.9 us -> 21.6 us
  Pallas kernels: 14.1 us -> 12.8 us
    all_to_all x1 -> x0, blocking collectives: 20.6 us -> none  [body(): lax.all_to_all(grads.reshape(count, 64, 1024), 'rows', 0, 0, tiled=True)]
    ppermute x1, waiting for transfers between devices: 0.01 us -> 5.81 us  [body(): from_above = lax.ppermute(down, 'rows', to_next)]
    all_to_all x1, starting transfers between devices: 5.86 us -> 11.1 us  [body(): lax.all_to_all(shares.reshape(every // 2, 8, 128), ('frames', 'rows'), 0,...]
    all_to_all x1, waiting for transfers between devices: 3.84 us -> 6.22 us  [body(): lax.all_to_all(shares.reshape(every // 2, 8, 128), ('frames', 'rows'), 0,...]
    ppermute x0 -> x1, starting transfers between devices: none -> 2.3 us  [body(): sent = lax.ppermute(sent, 'frames', pairs)]
    ppermute x0 -> x1, waiting for transfers between devices: none -> 1.51 us  [body(): sent = lax.ppermute(sent, 'frames', pairs)]
    ppermute x1, waiting for transfers between devices: 3.82 us -> 2.62 us  [body(): from_below = lax.ppermute(up, 'rows', to_last)]
  transfers between devices with their start and end apart: 5 -> 6, of which waited for: 3 -> 5; matrix products, arithmetic and copies ran while one was open for 0% -> 0% of each run, Pallas kernels for 3% -> 3%
where the time goes in v2:
time: 101 us; the launch traced here: 99.8 us
  blocking collectives  46.2 us (46%)
  starting transfers between devices  21.6 us (21%)
  waiting for transfers between devices  17.7 us (18%)
  Pallas kernels  12.8 us (13%)
    all_to_all x1, blocking collectives, body(): lax.all_to_all(place.reshape(64, 8, 128), 'frames', 0, 0, tiled=True)  29.9 us
    all_to_all x1, blocking collectives, body(): back = lax.all_to_all(back.reshape(64, 4, 128), 'frames', 0, 0, tiled=True)  16.2 us
    all_to_all x1, starting transfers between devices, body(): lax.all_to_all(shares.reshape(every // 2, 8, 128), ('frames', 'rows'), 0,...  11.1 us
    pallas_call x6, Pallas kernels, call(): pl.pallas_call(kernel, out_shape=outs, in_specs=[scalar] * smem + [local]...  11 us
    all_to_all x1, waiting for transfers between devices, body(): lax.all_to_all(shares.reshape(every // 2, 8, 128), ('frames', 'rows'), 0,...  6.22 us
    ppermute x1, waiting for transfers between devices, body(): from_above = lax.ppermute(down, 'rows', to_next)  5.81 us
    ppermute x1, starting transfers between devices, body(): above = lax.ppermute(own[256 - HALO:], 'rows', to_next)  4.02 us
    ppermute x1, waiting for transfers between devices, body(): from_below = lax.ppermute(up, 'rows', to_last)  2.62 us
  transfers between devices with their start and end apart: 6, of which 5 were waited for; matrix products, arithmetic and copies ran while one was open for 0% of the time, Pallas kernels for 3%

profile of v2, /device:TPU:1, one launch (start us, length us, event | category | flops | bytes accessed | tf_op | source)
XLA Modules:
  0.0 99.8 jit_solution(15291637742035315494)
XLA Ops:
  0.6 0.8 fusion
  1.4 4.0 %collective-permute-start = (bf16[48,256]{1,0:T(8,128)(2,1)S(1)}, bf16[48,256]{1,0:T(8,128)(2,1)S(1)}, u32[]{:S(2)}, u32[]{:S(2)}) collective-permute-start(bf16[48,256]{1,0:T(8,128)(2,1)S(1)} %bitcast.27), channel_id=1, source_target_pairs={{0,1},{1,2},{2,3},{3,4},{4,5},{5,6},{6,7},{8,9},{9,10},{10,11},{11... | collective-permute-start | bytes 73736 | tf_op jit(solution)/shard_map/ppermute | solution.py:506
  5.4 1.3 %collective-permute-start.1 = (bf16[48,256]{1,0:T(8,128)(2,1)S(1)}, bf16[48,256]{1,0:T(8,128)(2,1)S(1)}, u32[]{:S(2)}, u32[]{:S(2)}) collective-permute-start(bf16[48,256]{1,0:T(8,128)(2,1)S(1)} %bitcast.26), channel_id=1, source_target_pairs={{1,0},{2,1},{3,2},{4,3},{5,4},{6,5},{7,6},{9,8},{10,9},{11,10},{12... | collective-permute-start | bytes 73736 | tf_op jit(solution)/shard_map/ppermute | solution.py:507
  6.7 1.8 %shard_map.131 = (bf16[256,256]{1,0:T(8,128)(2,1)S(1)}, f32[1,256]{1,0:T(1,128)S(1)}, bf16[256,768]{1,0:T(8,128)(2,1)S(1)}, f32[1,4]{1,0:T(1,128)S(1)}, s32[16,1...) custom-call(bf16[256,256]{1,0:T(8,128)(2,1)} %bitcast.24, ...), custom_call_target="tpu_custom_call" | custom-call | flops 170000000 | bytes 5000000 | tf_op jit(solution)/shard_map/pallas_call | solution.py:477
  8.5 0.0 collective-permute-done.above
  8.5 1.5 %collective-permute-done.1.below = bf16[48,256]{1,0:T(8,128)(2,1)S(1)} collective-permute-done((bf16[48,256]{1,0:T(8,128)(2,1)S(1)}, bf16[48,256]{1,0:T(8,128)(2,1)S(1)}, u32[]{:S(2)}, u32[]{:S(2)}) %collective-permute-start.1) | collective-permute-done | bytes 24608 | tf_op jit(solution)/shard_map/ppermute | solution.py:507
  10.0 3.0 %shard_map.132 = (bf16[96,256]{1,0:T(8,128)(2,1)S(1)}, bf16[96,256]{1,0:T(8,128)(2,1)S(1)}, bf16[384,256]{1,0:T(8,128)(2,1)S(1)}, bf16[384,256]{1,0:T(8,128)(2,1...) custom-call(s32[1]{0:T(128)} %bitcast.1.rank, ...), custom_call_target="tpu_custom_call" | custom-call | tf_op jit(solution)/shard_map/pallas_call | solution.py:449
  13.0 29.9 %all_to_all.15 = bf16[64,8,128]{2,1,0:T(8,128)(2,1)S(1)} all-to-all(bf16[64,8,128]{2,1,0:T(8,128)(2,1)S(1)} %bitcast.22), channel_id=1, replica_groups=mesh['frames'=64,'rows'=8] {'frames'}, dimensions={0} | all-to-all | bytes 262144 | tf_op jit(solution)/shard_map/all_to_all | solution.py:565
  42.9 3.0 %shard_map.133 = (bf16[2048,128]{1,0:T(8,128)(2,1)S(1)}, bf16[256,128]{1,0:T(8,128)(2,1)S(1)}) custom-call(bf16[512,128]{1,0:T(8,128)(2,1)S(1)} %bitcast.20, f32[1,512]{1,0:T(1,128)S(1)} %get-tuple-element.50.gain, bf16[512,1536]{1,0:T(8,128)(2,1)S(1)} %get-tuple-element.51.attend, f32[1,8]{1,0:T(1,128)S(1)} %get-tuple-element.52.scale, ...), custom_call_target="tpu_custom_call" | custom-call | tf_op jit(solution)/shard_map/pallas_call | solution.py:449
  46.0 16.2 %all_to_all.16 = bf16[64,4,128]{2,1,0:T(4,128)(2,1)S(1)} all-to-all(bf16[64,4,128]{2,1,0:T(4,128)(2,1)S(1)} %bitcast.23), channel_id=1, replica_groups=mesh['frames'=64,'rows'=8] {'frames'}, dimensions={0} | all-to-all | bytes 131072 | tf_op jit(solution)/shard_map/all_to_all | solution.py:573
  62.2 2.3 %shard_map.134 = (bf16[2048,128]{1,0:T(8,128)(2,1)S(1)}, bf16[2048,128]{1,0:T(8,128)(2,1)S(1)}, bf16[48,512]{1,0:T(8,128)(2,1)S(1)}, bf16[48,512]{1,0:T(8,128)(2...) custom-call(s32[1]{0:T(128)} %bitcast.core, ...), custom_call_target="tpu_custom_call" | custom-call | tf_op jit(solution)/shard_map/pallas_call | solution.py:449
  64.5 2.3 %collective-permute-start.4 = (bf16[2048,128]{1,0:T(8,128)(2,1)S(1)}, bf16[2048,128]{1,0:T(8,128)(2,1)S(1)}, u32[]{:S(2)}, u32[]{:S(2)}) collective-permute-start(bf16[2048,128]{1,0:T(8,128)(2,1)S(1)} %get-tuple-element.74), channel_id=1, source_target_pairs={{0,8},{8,0},{16,24},{24,16},{32,40},{40,32},{48,56},{56,48},{64,72... | collective-permute-start | bytes 1572872 | tf_op jit(solution)/shard_map/ppermute | solution.py:606
  66.8 1.5 %collective-permute-done.4.sent = bf16[2048,128]{1,0:T(8,128)(2,1)S(1)} collective-permute-done((bf16[2048,128]{1,0:T(8,128)(2,1)S(1)}, bf16[2048,128]{1,0:T(8,128)(2,1)S(1)}, u32[]{:S(2)}, u32[]{:S(2)}) %collective-permute-start.4) | collective-permute-done | bytes 524320 | tf_op jit(solution)/shard_map/ppermute | solution.py:606
  68.3 0.9 shard_map.136
  69.2 11.1 %all-to-all-start.2 = ((bf16[256,8,128]{2,1,0:T(8,128)(2,1)}), bf16[256,8,128]{2,1,0:T(8,128)(2,1)S(1)}, u32[]{:S(2)}, u32[]{:S(2)}) async-start(bf16[256,8,128]{2,1,0:T(8,128)(2,1)} %bitcast.17), calls=%async_computation.2 | async-start | bytes 1048576 | tf_op jit(solution)/shard_map/all_to_all | solution.py:627
  80.4 1.6 %collective-permute-start.2 = (bf16[48,512]{1,0:T(8,128)(2,1)S(1)}, bf16[48,512]{1,0:T(8,128)(2,1)S(1)}, u32[]{:S(2)}, u32[]{:S(2)}) collective-permute-start(bf16[48,512]{1,0:T(8,128)(2,1)S(1)} %get-tuple-element.66), channel_id=1, source_target_pairs={{0,1},{1,2},{2,3},{3,4},{4,5},{5,6},{6,7},{8,9},{9,10},{10,11},{11... | collective-permute-start | bytes 147464 | tf_op jit(solution)/shard_map/ppermute | solution.py:608
  82.0 1.3 %collective-permute-start.3 = (bf16[48,512]{1,0:T(8,128)(2,1)S(1)}, bf16[48,512]{1,0:T(8,128)(2,1)S(1)}, u32[]{:S(2)}, u32[]{:S(2)}) collective-permute-start(bf16[48,512]{1,0:T(8,128)(2,1)S(1)} %get-tuple-element.67), channel_id=1, source_target_pairs={{1,0},{2,1},{3,2},{4,3},{5,4},{6,5},{7,6},{9,8},{10,9},{11,10},{12... | collective-permute-start | bytes 147464 | tf_op jit(solution)/shard_map/ppermute | solution.py:607
  83.3 5.8 %collective-permute-done.2.from_above = bf16[48,512]{1,0:T(8,128)(2,1)S(1)} collective-permute-done((bf16[48,512]{1,0:T(8,128)(2,1)S(1)}, bf16[48,512]{1,0:T(8,128)(2,1)S(1)}, u32[]{:S(2)}, u32[]{:S(2)}) %collective-permute-start.2) | collective-permute-done | bytes 49184 | tf_op jit(solution)/shard_map/ppermute | solution.py:608
  89.1 2.6 %collective-permute-done.3.from_below = bf16[48,512]{1,0:T(8,128)(2,1)S(1)} collective-permute-done((bf16[48,512]{1,0:T(8,128)(2,1)S(1)}, bf16[48,512]{1,0:T(8,128)(2,1)S(1)}, u32[]{:S(2)}, u32[]{:S(2)}) %collective-permute-start.3) | collective-permute-done | bytes 49184 | tf_op jit(solution)/shard_map/ppermute | solution.py:607
  91.7 1.2 %shard_map.135 = (bf16[256,256]{1,0:T(8,128)(2,1)}, f32[8,128]{1,0:T(8,128)S(1)}) custom-call(bf16[48,512]{1,0:T(8,128)(2,1)S(1)} %collective-permute-done.2.from_above, bf16[48,512]{1,0:T(8,128)(2,1)S(1)} %collective-permute-done.3.from_below, bf16[256,256]{1,0:T(8,128)(2,1)S(1)} %get-tuple-element.68.ct_query, ...), custom_call_target="tpu_custom_call" | custom-call | flops 170000000 | bytes 2000000 | tf_op jit(solution)/shard_map/pallas_call | solution.py:449
  92.9 6.2 %all-to-all-done.2.shares = bf16[256,8,128]{2,1,0:T(8,128)(2,1)S(1)} async-done(((bf16[256,8,128]{2,1,0:T(8,128)(2,1)}), bf16[256,8,128]{2,1,0:T(8,128)(2,1)S(1)}, u32[]{:S(2)}, u32[]{:S(2)}) %all-to-all-start.2) | async-done | bytes 524320 | tf_op jit(solution)/shard_map/all_to_all | solution.py:627
  99.1 0.7 shard_map.137
Async XLA Ops:
  1.4 7.1 %collective-permute-start = (bf16[48,256]{1,0:T(8,128)(2,1)S(1)}, bf16[48,256]{1,0:T(8,128)(2,1)S(1)}, u32[]{:S(2)}, u32[]{:S(2)}) collective-permute-start(bf16[48,256]{1,0:T(8,128)(2,1)S(1)} %bitcast.27), channel_id=1, source_target_pairs={{0,1},{1,2},{2,3},{3,4},{4,5},{5,6},{6,7},{8,9},{9,10},{10,11},{11... | collective-permute-start | bytes 73736 | tf_op jit(solution)/shard_map/ppermute | solution.py:506
  5.4 4.6 %collective-permute-start.1 = (bf16[48,256]{1,0:T(8,128)(2,1)S(1)}, bf16[48,256]{1,0:T(8,128)(2,1)S(1)}, u32[]{:S(2)}, u32[]{:S(2)}) collective-permute-start(bf16[48,256]{1,0:T(8,128)(2,1)S(1)} %bitcast.26), channel_id=1, source_target_pairs={{1,0},{2,1},{3,2},{4,3},{5,4},{6,5},{7,6},{9,8},{10,9},{11,10},{12... | collective-permute-start | bytes 73736 | tf_op jit(solution)/shard_map/ppermute | solution.py:507
  64.5 3.8 %collective-permute-start.4 = (bf16[2048,128]{1,0:T(8,128)(2,1)S(1)}, bf16[2048,128]{1,0:T(8,128)(2,1)S(1)}, u32[]{:S(2)}, u32[]{:S(2)}) collective-permute-start(bf16[2048,128]{1,0:T(8,128)(2,1)S(1)} %get-tuple-element.74), channel_id=1, source_target_pairs={{0,8},{8,0},{16,24},{24,16},{32,40},{40,32},{48,56},{56,48},{64,72... | collective-permute-start | bytes 1572872 | tf_op jit(solution)/shard_map/ppermute | solution.py:606
  69.2 29.9 %all-to-all-start.2 = ((bf16[256,8,128]{2,1,0:T(8,128)(2,1)}), bf16[256,8,128]{2,1,0:T(8,128)(2,1)S(1)}, u32[]{:S(2)}, u32[]{:S(2)}) async-start(bf16[256,8,128]{2,1,0:T(8,128)(2,1)} %bitcast.17), calls=%async_computation.2 | async-start | bytes 1048576 | tf_op jit(solution)/shard_map/all_to_all | solution.py:627
  80.4 8.7 %collective-permute-start.2 = (bf16[48,512]{1,0:T(8,128)(2,1)S(1)}, bf16[48,512]{1,0:T(8,128)(2,1)S(1)}, u32[]{:S(2)}, u32[]{:S(2)}) collective-permute-start(bf16[48,512]{1,0:T(8,128)(2,1)S(1)} %get-tuple-element.66), channel_id=1, source_target_pairs={{0,1},{1,2},{2,3},{3,4},{4,5},{5,6},{6,7},{8,9},{9,10},{10,11},{11... | collective-permute-start | bytes 147464 | tf_op jit(solution)/shard_map/ppermute | solution.py:608
  82.0 9.7 %collective-permute-start.3 = (bf16[48,512]{1,0:T(8,128)(2,1)S(1)}, bf16[48,512]{1,0:T(8,128)(2,1)S(1)}, u32[]{:S(2)}, u32[]{:S(2)}) collective-permute-start(bf16[48,512]{1,0:T(8,128)(2,1)S(1)} %get-tuple-element.67), channel_id=1, source_target_pairs={{1,0},{2,1},{3,2},{4,3},{5,4},{6,5},{7,6},{9,8},{10,9},{11,10},{12... | collective-permute-start | bytes 147464 | tf_op jit(solution)/shard_map/ppermute | solution.py:607

commit v3 on v2

--- a/solution.py
+++ b/solution.py
@@ -87,6 +87,28 @@
     return scale * ct - values * (scale * scale * scale * head_sum(ct * values, block))
 
 
+def ordering(size, target):
+    return zero_one(iota((size, target.shape[1]), 0) == target)
+
+
+def merge_order():
+    patch = iota((1, 256), 1)
+    group = ((patch >> 3) & 2) + (patch & 1)
+    return ordering(256, (group << 6) + ((patch >> 5) << 3) + ((patch >> 1) & 7))
+
+
+def bits(count):
+    return count.bit_length() - 1
+
+
+def lanes_to_rows_product(values):
+    count, blocks = values.shape[0], values.shape[1] // 128
+    stacked = jnp.concatenate([values[:, 128 * j : 128 * j + 128] for j in range(blocks)], axis=0)
+    at = iota((1, count * blocks), 1)
+    target = ((at & (count - 1)) << bits(blocks)) + (at >> bits(count))
+    return mm(ordering(count * blocks, target), stacked).astype(BF)
+
+
 def lanes_to_rows(values, rows, base):
     count, blocks = values.shape[0], values.shape[1] // 128
     for j in range(blocks):
@@ -100,22 +122,6 @@
 
 def merged_spots():
     return [[32 * a + 16 * (group >> 1) + (group & 1) for a in range(8)] for group in range(4)]
-
-
-def split_patches(mixed, rows, base):
-    for half in range(2):
-        at = base + 256 * half
-        rows[at : at + 256] = mixed[:, 128 * half : 128 * half + 128]
-    groups = []
-    for spots in merged_spots():
-        halves = [
-            jnp.concatenate(
-                [rows[pl.ds(base + 256 * half + spot, 8, stride=2), :] for spot in spots], axis=0
-            )
-            for half in range(2)
-        ]
-        groups.append(jnp.concatenate(halves, axis=1).astype(BF))
-    return groups
 
 
 def join_patches(groups, rows, base):
@@ -159,8 +165,8 @@
 def fine_forward(
     rank,
     core,
-    above,
-    below,
+    first,
+    second,
     query,
     own_keys,
     own_value,
@@ -171,31 +177,19 @@
     output,
     cotangent,
     merge,
-    gain_far,
-    attend_far,
-    scale_far,
-    output_far,
     beside_out,
     raw_out,
     key_out,
     value_out,
     prob_out,
     attn_out,
-    gain_out,
-    attend_out,
-    scale_out,
-    output_out,
     place_out,
-    rows,
-    sems,
 ):
-    far = (gain_far, attend_far, scale_far, output_far)
-    close = (gain_out, attend_out, scale_out, output_out)
-    copies = [pltpu.make_async_copy(far[at], close[at], sems.at[at]) for at in range(4)]
-    for copy in copies:
-        copy.start()
     del core
-    halo = jnp.concatenate([above[...], below[...]], axis=0).astype(F32)
+    is_even = (rank[0] & 1) == 0
+    above = jnp.where(is_even, second[...].astype(F32), first[...].astype(F32))
+    below = jnp.where(is_even, first[...].astype(F32), second[...].astype(F32))
+    halo = jnp.concatenate([above, below], axis=0)
     normed = rms(halo, gain[...])
     beside_out[...] = normed
     beside = mm(normed, attend[:, 256:]).astype(BF)
@@ -222,14 +216,12 @@
     attn = jnp.concatenate(parts, axis=0).astype(BF)
     attn_out[...] = attn
     mixed = (tokens[...].astype(F32) + mm(attn, output[...])).astype(BF)
-    patches = split_patches(mixed.astype(F32), rows, 0)
-    merged = mm(patches[0], merge[:256])
+    patches = mm(merge_order(), mixed).astype(BF)
+    merged = mm(patches[:64], merge[:256])
     for group in range(1, 4):
-        merged += mm(patches[group], merge[256 * group : 256 * group + 256])
-    lanes_to_rows(jnp.concatenate([merged, cotangent[...].astype(F32)], axis=1), rows, 512)
-    place_out[...] = rows[512:].astype(BF)
-    for copy in copies:
-        copy.wait()
+        merged += mm(patches[64 * group : 64 * group + 64], merge[256 * group : 256 * group + 256])
+    both = jnp.concatenate([merged.astype(BF), cotangent[...]], axis=1)
+    place_out[...] = lanes_to_rows_product(both)
 
 
 def coarse(place, gain, attend, scale, output, grad_out, back_out, rows, back_rows):
@@ -438,18 +430,13 @@
     return pltpu.VMEM(shape, dtype)
 
 
-def call(kernel, outs, *args, smem=0, far=0, scratch=(), cost=None):
-    close = len(args) - far
-    args = list(args[:close]) + [
-        pltpu.with_memory_space_constraint(arg, pltpu.HBM) for arg in args[close:]
-    ]
+def call(kernel, outs, *args, smem=0, scratch=(), cost=None):
     local = pl.BlockSpec(memory_space=pltpu.VMEM)
-    hbm = pl.BlockSpec(memory_space=pltpu.HBM)
     scalar = pl.BlockSpec(memory_space=pltpu.SMEM)
     return pl.pallas_call(
         kernel,
         out_shape=outs,
-        in_specs=[scalar] * smem + [local] * (close - smem) + [hbm] * far,
+        in_specs=[scalar] * smem + [local] * (len(args) - smem),
         scratch_shapes=scratch,
         out_specs=[local] * len(outs),
         compiler_params=pltpu.CompilerParams(vmem_limit_bytes=VMEM_BYTES),
@@ -503,13 +490,21 @@
     to_next = [(i, i + 1) for i in range(count - 1)]
     to_last = [(i + 1, i) for i in range(count - 1)]
     own = tokens.reshape(256, 256)
-    above = lax.ppermute(own[256 - HALO :], "rows", to_next)
-    below = lax.ppermute(own[:HALO], "rows", to_last)
+    place = lax.axis_index("rows")
+    is_even = (place & 1) == 0
+    top, bottom = own[:HALO], own[256 - HALO :]
+    first = lax.ppermute(
+        jnp.where(is_even, bottom, top), "rows", [(at, at ^ 1) for at in range(count)]
+    )
+    second = lax.ppermute(
+        jnp.where(is_even, top, bottom), "rows", [(at, ((at + 1) ^ 1) - 1) for at in range(1, count - 1)]
+    )
     rank = lax.axis_index("rows").astype(jnp.int32).reshape(1)
     core = (lax.axis_index("frames") & 1).astype(jnp.int32).reshape(1)
     square = (256, 256)
     (
         (own, gain_two, attend_two, scale_two, keep, output_two, cot, merge_weight),
+        three,
         (normed, raw_query, raw_key, query, own_keys, own_value),
     ) = split(
         fetch_and_call(
@@ -524,14 +519,17 @@
             output_two,
             cotangent.reshape(64, 512),
             merge_weight,
+            gain_three.reshape(1, 512),
+            attend_three,
+            scale_three.reshape(1, 8),
+            output_three,
             cost=pl.CostEstimate(flops=170_000_000, bytes_accessed=5_000_000, transcendentals=0),
         ),
         8,
+        4,
         6,
     )
-    gain_three, scale_three = gain_three.reshape(1, 512), scale_three.reshape(1, 8)
-    three = (gain_three, attend_three, scale_three, output_three)
-    normed_beside, raw_beside, keys, value, prob, attn, *three, place = call(
+    normed_beside, raw_beside, keys, value, prob, attn, place = call(
         fine_forward,
         [
             near((96, 256)),
@@ -540,13 +538,12 @@
             near((384, 256)),
             near((2, 256, 512)),
             near(square),
-            *[near(weight.shape, weight.dtype) for weight in three],
             jax.ShapeDtypeStruct((512, 128), BF),
         ],
         rank,
         core,
-        above,
-        below,
+        first,
+        second,
         query,
         own_keys,
         own_value,
@@ -557,10 +554,7 @@
         output_two,
         cot,
         merge_weight,
-        *three,
         smem=2,
-        far=4,
-        scratch=[pltpu.VMEM((1024, 128), F32), pltpu.SemaphoreType.DMA((4,))],
     )
     place = lax.all_to_all(place.reshape(64, 8, 128), "frames", 0, 0, tiled=True)
     grad_three, back = call(

time: 101 us -> 100 us (0.990)
  starting transfers between devices: 21.6 us -> 23.5 us
  waiting for transfers between devices: 17.7 us -> 16.2 us
  blocking collectives: 46.2 us -> 44.8 us
    all_to_all x1, starting transfers between devices: 11.1 us -> 13.6 us  [body(): lax.all_to_all(shares.reshape(every // 2, 8, 128), ('frames', 'rows'), 0,...]
    ppermute x2, waiting for transfers between devices: 1.48 us -> 0.01 us  [the longest x1 0.01 us: body(): lax.ppermute(jnp.where(is_even, bottom, top), 'rows', [(at, at ^ 1) for a...]
    all_to_all x1, blocking collectives: 29.9 us -> 28.6 us  [body(): lax.all_to_all(place.reshape(64, 8, 128), 'frames', 0, 0, tiled=True)]
  transfers between devices with their start and end apart: 6 -> 6, of which waited for: 5 -> 4; matrix products, arithmetic and copies ran while one was open for 0% -> 0% of each run, Pallas kernels for 3% -> 4%
where the time goes in v3:
time: 100 us; the launch traced here: 98.6 us
  blocking collectives  44.8 us (45%)
  starting transfers between devices  23.5 us (24%)
  waiting for transfers between devices  16.2 us (16%)
  Pallas kernels  12.6 us (13%)
    all_to_all x1, blocking collectives, body(): lax.all_to_all(place.reshape(64, 8, 128), 'frames', 0, 0, tiled=True)  28.6 us
    all_to_all x1, blocking collectives, body(): back = lax.all_to_all(back.reshape(64, 4, 128), 'frames', 0, 0, tiled=True)  16.2 us
    all_to_all x1, starting transfers between devices, body(): lax.all_to_all(shares.reshape(every // 2, 8, 128), ('frames', 'rows'), 0,...  13.6 us
    pallas_call x6, Pallas kernels, call(): pl.pallas_call(kernel, out_shape=outs, in_specs=[scalar] * smem + [local]...  10.3 us
    all_to_all x1, waiting for transfers between devices, body(): lax.all_to_all(shares.reshape(every // 2, 8, 128), ('frames', 'rows'), 0,...  6.22 us
    ppermute x1, waiting for transfers between devices, body(): from_above = lax.ppermute(down, 'rows', to_next)  5.81 us
    ppermute x1, starting transfers between devices, body(): lax.ppermute(jnp.where(is_even, bottom, top), 'rows', [(at, at ^ 1) for a...  4.02 us
    ppermute x1, waiting for transfers between devices, body(): from_below = lax.ppermute(up, 'rows', to_last)  2.62 us
  transfers between devices with their start and end apart: 6, of which 4 were waited for; matrix products, arithmetic and copies ran while one was open for 0% of the time, Pallas kernels for 4%

profile of v3, /device:TPU:1, one launch (start us, length us, event | category | flops | bytes accessed | tf_op | source)
XLA Modules:
  0.0 98.6 jit_solution(7442827856628487749)
XLA Ops:
  0.6 0.8 broadcast_select_fusion
  1.4 4.0 %collective-permute-start = (bf16[48,256]{1,0:T(8,128)(2,1)S(1)}, bf16[48,256]{1,0:T(8,128)(2,1)S(1)}, u32[]{:S(2)}, u32[]{:S(2)}) collective-permute-start(bf16[48,256]{1,0:T(8,128)(2,1)S(1)} %bitcast.27), channel_id=1, source_target_pairs={{0,1},{1,0},{2,3},{3,2},{4,5},{5,4},{6,7},{7,6},{8,9},{9,8},{10,11... | collective-permute-start | bytes 73736 | tf_op jit(solution)/shard_map/ppermute | solution.py:496
  5.4 0.7 collective-permute-start.1
  6.1 2.3 %shard_map.131 = (bf16[256,256]{1,0:T(8,128)(2,1)S(1)}, f32[1,256]{1,0:T(1,128)S(1)}, bf16[256,768]{1,0:T(8,128)(2,1)S(1)}, f32[1,4]{1,0:T(1,128)S(1)}, s32[16,1...) custom-call(bf16[256,256]{1,0:T(8,128)(2,1)} %bitcast.24, ...), custom_call_target="tpu_custom_call" | custom-call | flops 170000000 | bytes 5000000 | tf_op jit(solution)/shard_map/pallas_call | solution.py:464
  8.4 0.0 collective-permute-done.first
  8.4 0.0 collective-permute-done.1.second
  8.4 2.2 %shard_map.132 = (bf16[96,256]{1,0:T(8,128)(2,1)S(1)}, bf16[96,256]{1,0:T(8,128)(2,1)S(1)}, bf16[384,256]{1,0:T(8,128)(2,1)S(1)}, bf16[384,256]{1,0:T(8,128)(2,1...) custom-call(s32[1]{0:T(128)} %bitcast.1.rank, s32[1]{0:T(128)} %bitcast.core, ...), custom_call_target="tpu_custom_call" | custom-call | tf_op jit(solution)/shard_map/pallas_call | solution.py:436
  10.7 28.6 %all_to_all.15 = bf16[64,8,128]{2,1,0:T(8,128)(2,1)S(1)} all-to-all(bf16[64,8,128]{2,1,0:T(8,128)(2,1)S(1)} %bitcast.22), channel_id=1, replica_groups=mesh['frames'=64,'rows'=8] {'frames'}, dimensions={0} | all-to-all | bytes 262144 | tf_op jit(solution)/shard_map/all_to_all | solution.py:559
  39.3 3.0 %shard_map.133 = (bf16[2048,128]{1,0:T(8,128)(2,1)S(1)}, bf16[256,128]{1,0:T(8,128)(2,1)S(1)}) custom-call(bf16[512,128]{1,0:T(8,128)(2,1)S(1)} %bitcast.20, f32[1,512]{1,0:T(1,128)S(1)} %get-tuple-element.50.gain, bf16[512,1536]{1,0:T(8,128)(2,1)S(1)} %get-tuple-element.51.attend, f32[1,8]{1,0:T(1,128)S(1)} %get-tuple-element.52.scale, ...), custom_call_target="tpu_custom_call" | custom-call | tf_op jit(solution)/shard_map/pallas_call | solution.py:436
  42.3 16.2 %all_to_all.16 = bf16[64,4,128]{2,1,0:T(4,128)(2,1)S(1)} all-to-all(bf16[64,4,128]{2,1,0:T(4,128)(2,1)S(1)} %bitcast.23), channel_id=1, replica_groups=mesh['frames'=64,'rows'=8] {'frames'}, dimensions={0} | all-to-all | bytes 131072 | tf_op jit(solution)/shard_map/all_to_all | solution.py:567
  58.5 2.3 %shard_map.134 = (bf16[2048,128]{1,0:T(8,128)(2,1)S(1)}, bf16[2048,128]{1,0:T(8,128)(2,1)S(1)}, bf16[48,512]{1,0:T(8,128)(2,1)S(1)}, bf16[48,512]{1,0:T(8,128)(2...) custom-call(s32[1]{0:T(128)} %bitcast.core, ...), custom_call_target="tpu_custom_call" | custom-call | tf_op jit(solution)/shard_map/pallas_call | solution.py:436
  60.8 2.3 %collective-permute-start.4 = (bf16[2048,128]{1,0:T(8,128)(2,1)S(1)}, bf16[2048,128]{1,0:T(8,128)(2,1)S(1)}, u32[]{:S(2)}, u32[]{:S(2)}) collective-permute-start(bf16[2048,128]{1,0:T(8,128)(2,1)S(1)} %get-tuple-element.74), channel_id=1, source_target_pairs={{0,8},{8,0},{16,24},{24,16},{32,40},{40,32},{48,56},{56,48},{64,72... | collective-permute-start | bytes 1572872 | tf_op jit(solution)/shard_map/ppermute | solution.py:600
  63.1 1.5 %collective-permute-done.4.sent = bf16[2048,128]{1,0:T(8,128)(2,1)S(1)} collective-permute-done((bf16[2048,128]{1,0:T(8,128)(2,1)S(1)}, bf16[2048,128]{1,0:T(8,128)(2,1)S(1)}, u32[]{:S(2)}, u32[]{:S(2)}) %collective-permute-start.4) | collective-permute-done | bytes 524320 | tf_op jit(solution)/shard_map/ppermute | solution.py:600
  64.6 0.9 shard_map.136
  65.5 13.6 %all-to-all-start.2 = ((bf16[256,8,128]{2,1,0:T(8,128)(2,1)}), bf16[256,8,128]{2,1,0:T(8,128)(2,1)S(1)}, u32[]{:S(2)}, u32[]{:S(2)}) async-start(bf16[256,8,128]{2,1,0:T(8,128)(2,1)} %bitcast.17), calls=%async_computation.2 | async-start | bytes 1048576 | tf_op jit(solution)/shard_map/all_to_all | solution.py:621
  79.2 1.6 %collective-permute-start.2 = (bf16[48,512]{1,0:T(8,128)(2,1)S(1)}, bf16[48,512]{1,0:T(8,128)(2,1)S(1)}, u32[]{:S(2)}, u32[]{:S(2)}) collective-permute-start(bf16[48,512]{1,0:T(8,128)(2,1)S(1)} %get-tuple-element.66), channel_id=1, source_target_pairs={{0,1},{1,2},{2,3},{3,4},{4,5},{5,6},{6,7},{8,9},{9,10},{10,11},{11... | collective-permute-start | bytes 147464 | tf_op jit(solution)/shard_map/ppermute | solution.py:602
  80.8 1.3 %collective-permute-start.3 = (bf16[48,512]{1,0:T(8,128)(2,1)S(1)}, bf16[48,512]{1,0:T(8,128)(2,1)S(1)}, u32[]{:S(2)}, u32[]{:S(2)}) collective-permute-start(bf16[48,512]{1,0:T(8,128)(2,1)S(1)} %get-tuple-element.67), channel_id=1, source_target_pairs={{1,0},{2,1},{3,2},{4,3},{5,4},{6,5},{7,6},{9,8},{10,9},{11,10},{12... | collective-permute-start | bytes 147464 | tf_op jit(solution)/shard_map/ppermute | solution.py:601
  82.1 5.8 %collective-permute-done.2.from_above = bf16[48,512]{1,0:T(8,128)(2,1)S(1)} collective-permute-done((bf16[48,512]{1,0:T(8,128)(2,1)S(1)}, bf16[48,512]{1,0:T(8,128)(2,1)S(1)}, u32[]{:S(2)}, u32[]{:S(2)}) %collective-permute-start.2) | collective-permute-done | bytes 49184 | tf_op jit(solution)/shard_map/ppermute | solution.py:602
  87.9 2.6 %collective-permute-done.3.from_below = bf16[48,512]{1,0:T(8,128)(2,1)S(1)} collective-permute-done((bf16[48,512]{1,0:T(8,128)(2,1)S(1)}, bf16[48,512]{1,0:T(8,128)(2,1)S(1)}, u32[]{:S(2)}, u32[]{:S(2)}) %collective-permute-start.3) | collective-permute-done | bytes 49184 | tf_op jit(solution)/shard_map/ppermute | solution.py:601
  90.5 1.2 %shard_map.135 = (bf16[256,256]{1,0:T(8,128)(2,1)}, f32[8,128]{1,0:T(8,128)S(1)}) custom-call(bf16[48,512]{1,0:T(8,128)(2,1)S(1)} %collective-permute-done.2.from_above, bf16[48,512]{1,0:T(8,128)(2,1)S(1)} %collective-permute-done.3.from_below, bf16[256,256]{1,0:T(8,128)(2,1)S(1)} %get-tuple-element.68.ct_query, ...), custom_call_target="tpu_custom_call" | custom-call | flops 170000000 | bytes 2000000 | tf_op jit(solution)/shard_map/pallas_call | solution.py:436
  91.7 6.2 %all-to-all-done.2.shares = bf16[256,8,128]{2,1,0:T(8,128)(2,1)S(1)} async-done(((bf16[256,8,128]{2,1,0:T(8,128)(2,1)}), bf16[256,8,128]{2,1,0:T(8,128)(2,1)S(1)}, u32[]{:S(2)}, u32[]{:S(2)}) %all-to-all-start.2) | async-done | bytes 524320 | tf_op jit(solution)/shard_map/all_to_all | solution.py:621
  97.9 0.7 shard_map.137
Async XLA Ops:
  1.4 7.0 %collective-permute-start = (bf16[48,256]{1,0:T(8,128)(2,1)S(1)}, bf16[48,256]{1,0:T(8,128)(2,1)S(1)}, u32[]{:S(2)}, u32[]{:S(2)}) collective-permute-start(bf16[48,256]{1,0:T(8,128)(2,1)S(1)} %bitcast.27), channel_id=1, source_target_pairs={{0,1},{1,0},{2,3},{3,2},{4,5},{5,4},{6,7},{7,6},{8,9},{9,8},{10,11... | collective-permute-start | bytes 73736 | tf_op jit(solution)/shard_map/ppermute | solution.py:496
  5.4 3.0 %collective-permute-start.1 = (bf16[48,256]{1,0:T(8,128)(2,1)S(1)}, bf16[48,256]{1,0:T(8,128)(2,1)S(1)}, u32[]{:S(2)}, u32[]{:S(2)}) collective-permute-start(bf16[48,256]{1,0:T(8,128)(2,1)S(1)} %bitcast.26), channel_id=1, source_target_pairs={{1,2},{2,1},{3,4},{4,3},{5,6},{6,5},{9,10},{10,9},{11,12},{12,11},... | collective-permute-start | bytes 73736 | tf_op jit(solution)/shard_map/ppermute | solution.py:499
  60.8 3.8 %collective-permute-start.4 = (bf16[2048,128]{1,0:T(8,128)(2,1)S(1)}, bf16[2048,128]{1,0:T(8,128)(2,1)S(1)}, u32[]{:S(2)}, u32[]{:S(2)}) collective-permute-start(bf16[2048,128]{1,0:T(8,128)(2,1)S(1)} %get-tuple-element.74), channel_id=1, source_target_pairs={{0,8},{8,0},{16,24},{24,16},{32,40},{40,32},{48,56},{56,48},{64,72... | collective-permute-start | bytes 1572872 | tf_op jit(solution)/shard_map/ppermute | solution.py:600
  65.5 32.4 %all-to-all-start.2 = ((bf16[256,8,128]{2,1,0:T(8,128)(2,1)}), bf16[256,8,128]{2,1,0:T(8,128)(2,1)S(1)}, u32[]{:S(2)}, u32[]{:S(2)}) async-start(bf16[256,8,128]{2,1,0:T(8,128)(2,1)} %bitcast.17), calls=%async_computation.2 | async-start | bytes 1048576 | tf_op jit(solution)/shard_map/all_to_all | solution.py:621
  79.2 8.7 %collective-permute-start.2 = (bf16[48,512]{1,0:T(8,128)(2,1)S(1)}, bf16[48,512]{1,0:T(8,128)(2,1)S(1)}, u32[]{:S(2)}, u32[]{:S(2)}) collective-permute-start(bf16[48,512]{1,0:T(8,128)(2,1)S(1)} %get-tuple-element.66), channel_id=1, source_target_pairs={{0,1},{1,2},{2,3},{3,4},{4,5},{5,6},{6,7},{8,9},{9,10},{10,11},{11... | collective-permute-start | bytes 147464 | tf_op jit(solution)/shard_map/ppermute | solution.py:602
  80.8 9.7 %collective-permute-start.3 = (bf16[48,512]{1,0:T(8,128)(2,1)S(1)}, bf16[48,512]{1,0:T(8,128)(2,1)S(1)}, u32[]{:S(2)}, u32[]{:S(2)}) collective-permute-start(bf16[48,512]{1,0:T(8,128)(2,1)S(1)} %get-tuple-element.67), channel_id=1, source_target_pairs={{1,0},{2,1},{3,2},{4,3},{5,4},{6,5},{7,6},{9,8},{10,9},{11,10},{12... | collective-permute-start | bytes 147464 | tf_op jit(solution)/shard_map/ppermute | solution.py:601

commit v4 on v3

--- a/solution.py
+++ b/solution.py
@@ -99,14 +99,6 @@
 
 def bits(count):
     return count.bit_length() - 1
-
-
-def lanes_to_rows_product(values):
-    count, blocks = values.shape[0], values.shape[1] // 128
-    stacked = jnp.concatenate([values[:, 128 * j : 128 * j + 128] for j in range(blocks)], axis=0)
-    at = iota((1, count * blocks), 1)
-    target = ((at & (count - 1)) << bits(blocks)) + (at >> bits(count))
-    return mm(ordering(count * blocks, target), stacked).astype(BF)
 
 
 def lanes_to_rows(values, rows, base):
@@ -184,6 +176,7 @@
     prob_out,
     attn_out,
     place_out,
+    rows,
 ):
     del core
     is_even = (rank[0] & 1) == 0
@@ -220,8 +213,8 @@
     merged = mm(patches[:64], merge[:256])
     for group in range(1, 4):
         merged += mm(patches[64 * group : 64 * group + 64], merge[256 * group : 256 * group + 256])
-    both = jnp.concatenate([merged.astype(BF), cotangent[...]], axis=1)
-    place_out[...] = lanes_to_rows_product(both)
+    lanes_to_rows(jnp.concatenate([merged, cotangent[...].astype(F32)], axis=1), rows, 0)
+    place_out[...] = rows[...].astype(BF)
 
 
 def coarse(place, gain, attend, scale, output, grad_out, back_out, rows, back_rows):
@@ -236,23 +229,30 @@
     value = triple[:, 1024:]
     query = (unit(query_raw, block) * lanes).astype(BF)
     keys = unit(key_raw, block).astype(BF)
-    query_heads = split_heads(query, 8)
-    weight = jnp.exp(mm_nt(keys, query_heads))
-    prob = weight / jnp.sum(weight, axis=0, keepdims=True)
-    prob_half = prob.astype(BF)
-    attn = join_heads(mm_tn(prob_half, value), 8).astype(BF)
+    ct_attn = mm_nt(target, output[...]).astype(BF)
+    attns, ct_queries, ct_keys, ct_values = [], [], [], []
+    for at in (0, 256):
+        part = slice(at, at + 256)
+        query_heads = split_heads(query[:, part], 4)
+        weight = jnp.exp(mm_nt(keys[:, part], query_heads))
+        prob = weight / jnp.sum(weight, axis=0, keepdims=True)
+        prob_half = prob.astype(BF)
+        attns.append(join_heads(mm_tn(prob_half, value[:, part]), 4).astype(BF))
+        ct_heads = split_heads(ct_attn[:, part], 4)
+        ct_prob = mm_nt(value[:, part], ct_heads)
+        ct_score = prob * (ct_prob - jnp.sum(ct_prob * prob, axis=0, keepdims=True))
+        ct_score = ct_score.astype(BF)
+        ct_queries.append(join_heads(mm_tn(ct_score, keys[:, part]), 4))
+        ct_keys.append(mm(ct_score, query_heads))
+        ct_values.append(mm(prob_half, ct_heads))
+    attn = jnp.concatenate(attns, axis=1)
+    ct_query = jnp.concatenate(ct_queries, axis=1)
+    ct_key = jnp.concatenate(ct_keys, axis=1)
+    ct_value = jnp.concatenate(ct_values, axis=1).astype(BF)
     grad = mm_tn(attn, target)
     for part in range(4):
         rows[pl.ds(part, 512, stride=4), :] = grad[:, 128 * part : 128 * part + 128]
     grad_out[...] = rows[...].astype(BF)
-    ct_attn = mm_nt(target, output[...]).astype(BF)
-    ct_heads = split_heads(ct_attn, 8)
-    ct_prob = mm_nt(value, ct_heads)
-    ct_score = prob * (ct_prob - jnp.sum(ct_prob * prob, axis=0, keepdims=True))
-    ct_score = ct_score.astype(BF)
-    ct_query = join_heads(mm_tn(ct_score, keys), 8).astype(BF).astype(F32)
-    ct_key = mm(ct_score, query_heads).astype(BF).astype(F32)
-    ct_value = mm(prob_half, ct_heads).astype(BF)
     ct_triple = jnp.concatenate(
         [
             unit_back(query_raw, ct_query * lanes, block).astype(BF),
@@ -555,6 +555,7 @@
         cot,
         merge_weight,
         smem=2,
+        scratch=[pltpu.VMEM((512, 128), F32)],
     )
     place = lax.all_to_all(place.reshape(64, 8, 128), "frames", 0, 0, tiled=True)
     grad_three, back = call(

time: 100 us -> 99 us (0.990)
  Pallas kernels: 12.6 us -> 11.6 us
where the time goes in v4:
time: 99 us; the launch traced here: 97.6 us
  blocking collectives  44.8 us (45%)
  starting transfers between devices  23.5 us (24%)
  waiting for transfers between devices  16.2 us (16%)
  Pallas kernels  11.6 us (12%)
    all_to_all x1, blocking collectives, body(): lax.all_to_all(place.reshape(64, 8, 128), 'frames', 0, 0, tiled=True)  28.6 us
    all_to_all x1, blocking collectives, body(): back = lax.all_to_all(back.reshape(64, 4, 128), 'frames', 0, 0, tiled=True)  16.2 us
    all_to_all x1, starting transfers between devices, body(): lax.all_to_all(shares.reshape(every // 2, 8, 128), ('frames', 'rows'), 0,...  13.6 us
    pallas_call x6, Pallas kernels, call(): pl.pallas_call(kernel, out_shape=outs, in_specs=[scalar] * smem + [local]...  9.27 us
    all_to_all x1, waiting for transfers between devices, body(): lax.all_to_all(shares.reshape(every // 2, 8, 128), ('frames', 'rows'), 0,...  6.22 us
    ppermute x1, waiting for transfers between devices, body(): from_above = lax.ppermute(down, 'rows', to_next)  5.81 us
    ppermute x1, starting transfers between devices, body(): lax.ppermute(jnp.where(is_even, bottom, top), 'rows', [(at, at ^ 1) for a...  4.02 us
    ppermute x1, waiting for transfers between devices, body(): from_below = lax.ppermute(up, 'rows', to_last)  2.62 us
  transfers between devices with their start and end apart: 6, of which 4 were waited for; matrix products, arithmetic and copies ran while one was open for 0% of the time, Pallas kernels for 4%

profile of v4, /device:TPU:1, one launch (start us, length us, event | category | flops | bytes accessed | tf_op | source)
XLA Modules:
  0.0 97.6 jit_solution(5623535191535183777)
XLA Ops:
  0.6 0.8 broadcast_select_fusion
  1.4 4.0 %collective-permute-start = (bf16[48,256]{1,0:T(8,128)(2,1)S(1)}, bf16[48,256]{1,0:T(8,128)(2,1)S(1)}, u32[]{:S(2)}, u32[]{:S(2)}) collective-permute-start(bf16[48,256]{1,0:T(8,128)(2,1)S(1)} %bitcast.27), channel_id=1, source_target_pairs={{0,1},{1,0},{2,3},{3,2},{4,5},{5,4},{6,7},{7,6},{8,9},{9,8},{10,11... | collective-permute-start | bytes 73736 | tf_op jit(solution)/shard_map/ppermute | solution.py:496
  5.4 0.7 collective-permute-start.1
  6.1 2.3 %shard_map.131 = (bf16[256,256]{1,0:T(8,128)(2,1)S(1)}, f32[1,256]{1,0:T(1,128)S(1)}, bf16[256,768]{1,0:T(8,128)(2,1)S(1)}, f32[1,4]{1,0:T(1,128)S(1)}, s32[16,1...) custom-call(bf16[256,256]{1,0:T(8,128)(2,1)} %bitcast.24, ...), custom_call_target="tpu_custom_call" | custom-call | flops 170000000 | bytes 5000000 | tf_op jit(solution)/shard_map/pallas_call | solution.py:464
  8.4 0.0 collective-permute-done.first
  8.4 0.0 collective-permute-done.1.second
  8.4 1.6 %shard_map.132 = (bf16[96,256]{1,0:T(8,128)(2,1)S(1)}, bf16[96,256]{1,0:T(8,128)(2,1)S(1)}, bf16[384,256]{1,0:T(8,128)(2,1)S(1)}, bf16[384,256]{1,0:T(8,128)(2,1...) custom-call(s32[1]{0:T(128)} %bitcast.1.rank, s32[1]{0:T(128)} %bitcast.core, ...), custom_call_target="tpu_custom_call" | custom-call | tf_op jit(solution)/shard_map/pallas_call | solution.py:436
  10.1 28.6 %all_to_all.15 = bf16[64,8,128]{2,1,0:T(8,128)(2,1)S(1)} all-to-all(bf16[64,8,128]{2,1,0:T(8,128)(2,1)S(1)} %bitcast.22), channel_id=1, replica_groups=mesh['frames'=64,'rows'=8] {'frames'}, dimensions={0} | all-to-all | bytes 262144 | tf_op jit(solution)/shard_map/all_to_all | solution.py:560
  38.7 2.6 %shard_map.133 = (bf16[2048,128]{1,0:T(8,128)(2,1)S(1)}, bf16[256,128]{1,0:T(8,128)(2,1)S(1)}) custom-call(bf16[512,128]{1,0:T(8,128)(2,1)S(1)} %bitcast.20, f32[1,512]{1,0:T(1,128)S(1)} %get-tuple-element.50.gain, bf16[512,1536]{1,0:T(8,128)(2,1)S(1)} %get-tuple-element.51.attend, f32[1,8]{1,0:T(1,128)S(1)} %get-tuple-element.52.scale, ...), custom_call_target="tpu_custom_call" | custom-call | tf_op jit(solution)/shard_map/pallas_call | solution.py:436
  41.3 16.2 %all_to_all.16 = bf16[64,4,128]{2,1,0:T(4,128)(2,1)S(1)} all-to-all(bf16[64,4,128]{2,1,0:T(4,128)(2,1)S(1)} %bitcast.23), channel_id=1, replica_groups=mesh['frames'=64,'rows'=8] {'frames'}, dimensions={0} | all-to-all | bytes 131072 | tf_op jit(solution)/shard_map/all_to_all | solution.py:568
  57.5 2.3 %shard_map.134 = (bf16[2048,128]{1,0:T(8,128)(2,1)S(1)}, bf16[2048,128]{1,0:T(8,128)(2,1)S(1)}, bf16[48,512]{1,0:T(8,128)(2,1)S(1)}, bf16[48,512]{1,0:T(8,128)(2...) custom-call(s32[1]{0:T(128)} %bitcast.core, ...), custom_call_target="tpu_custom_call" | custom-call | tf_op jit(solution)/shard_map/pallas_call | solution.py:436
  59.8 2.3 %collective-permute-start.4 = (bf16[2048,128]{1,0:T(8,128)(2,1)S(1)}, bf16[2048,128]{1,0:T(8,128)(2,1)S(1)}, u32[]{:S(2)}, u32[]{:S(2)}) collective-permute-start(bf16[2048,128]{1,0:T(8,128)(2,1)S(1)} %get-tuple-element.74), channel_id=1, source_target_pairs={{0,8},{8,0},{16,24},{24,16},{32,40},{40,32},{48,56},{56,48},{64,72... | collective-permute-start | bytes 1572872 | tf_op jit(solution)/shard_map/ppermute | solution.py:601
  62.1 1.5 %collective-permute-done.4.sent = bf16[2048,128]{1,0:T(8,128)(2,1)S(1)} collective-permute-done((bf16[2048,128]{1,0:T(8,128)(2,1)S(1)}, bf16[2048,128]{1,0:T(8,128)(2,1)S(1)}, u32[]{:S(2)}, u32[]{:S(2)}) %collective-permute-start.4) | collective-permute-done | bytes 524320 | tf_op jit(solution)/shard_map/ppermute | solution.py:601
  63.6 0.9 shard_map.136
  64.6 13.6 %all-to-all-start.2 = ((bf16[256,8,128]{2,1,0:T(8,128)(2,1)}), bf16[256,8,128]{2,1,0:T(8,128)(2,1)S(1)}, u32[]{:S(2)}, u32[]{:S(2)}) async-start(bf16[256,8,128]{2,1,0:T(8,128)(2,1)} %bitcast.17), calls=%async_computation.2 | async-start | bytes 1048576 | tf_op jit(solution)/shard_map/all_to_all | solution.py:622
  78.2 1.6 %collective-permute-start.2 = (bf16[48,512]{1,0:T(8,128)(2,1)S(1)}, bf16[48,512]{1,0:T(8,128)(2,1)S(1)}, u32[]{:S(2)}, u32[]{:S(2)}) collective-permute-start(bf16[48,512]{1,0:T(8,128)(2,1)S(1)} %get-tuple-element.66), channel_id=1, source_target_pairs={{0,1},{1,2},{2,3},{3,4},{4,5},{5,6},{6,7},{8,9},{9,10},{10,11},{11... | collective-permute-start | bytes 147464 | tf_op jit(solution)/shard_map/ppermute | solution.py:603
  79.8 1.3 %collective-permute-start.3 = (bf16[48,512]{1,0:T(8,128)(2,1)S(1)}, bf16[48,512]{1,0:T(8,128)(2,1)S(1)}, u32[]{:S(2)}, u32[]{:S(2)}) collective-permute-start(bf16[48,512]{1,0:T(8,128)(2,1)S(1)} %get-tuple-element.67), channel_id=1, source_target_pairs={{1,0},{2,1},{3,2},{4,3},{5,4},{6,5},{7,6},{9,8},{10,9},{11,10},{12... | collective-permute-start | bytes 147464 | tf_op jit(solution)/shard_map/ppermute | solution.py:602
  81.1 5.8 %collective-permute-done.2.from_above = bf16[48,512]{1,0:T(8,128)(2,1)S(1)} collective-permute-done((bf16[48,512]{1,0:T(8,128)(2,1)S(1)}, bf16[48,512]{1,0:T(8,128)(2,1)S(1)}, u32[]{:S(2)}, u32[]{:S(2)}) %collective-permute-start.2) | collective-permute-done | bytes 49184 | tf_op jit(solution)/shard_map/ppermute | solution.py:603
  86.9 2.6 %collective-permute-done.3.from_below = bf16[48,512]{1,0:T(8,128)(2,1)S(1)} collective-permute-done((bf16[48,512]{1,0:T(8,128)(2,1)S(1)}, bf16[48,512]{1,0:T(8,128)(2,1)S(1)}, u32[]{:S(2)}, u32[]{:S(2)}) %collective-permute-start.3) | collective-permute-done | bytes 49184 | tf_op jit(solution)/shard_map/ppermute | solution.py:602
  89.5 1.2 %shard_map.135 = (bf16[256,256]{1,0:T(8,128)(2,1)}, f32[8,128]{1,0:T(8,128)S(1)}) custom-call(bf16[48,512]{1,0:T(8,128)(2,1)S(1)} %collective-permute-done.2.from_above, bf16[48,512]{1,0:T(8,128)(2,1)S(1)} %collective-permute-done.3.from_below, bf16[256,256]{1,0:T(8,128)(2,1)S(1)} %get-tuple-element.68.ct_query, ...), custom_call_target="tpu_custom_call" | custom-call | flops 170000000 | bytes 2000000 | tf_op jit(solution)/shard_map/pallas_call | solution.py:436
  90.7 6.2 %all-to-all-done.2.shares = bf16[256,8,128]{2,1,0:T(8,128)(2,1)S(1)} async-done(((bf16[256,8,128]{2,1,0:T(8,128)(2,1)}), bf16[256,8,128]{2,1,0:T(8,128)(2,1)S(1)}, u32[]{:S(2)}, u32[]{:S(2)}) %all-to-all-start.2) | async-done | bytes 524320 | tf_op jit(solution)/shard_map/all_to_all | solution.py:622
  96.9 0.7 shard_map.137
Async XLA Ops:
  1.4 7.0 %collective-permute-start = (bf16[48,256]{1,0:T(8,128)(2,1)S(1)}, bf16[48,256]{1,0:T(8,128)(2,1)S(1)}, u32[]{:S(2)}, u32[]{:S(2)}) collective-permute-start(bf16[48,256]{1,0:T(8,128)(2,1)S(1)} %bitcast.27), channel_id=1, source_target_pairs={{0,1},{1,0},{2,3},{3,2},{4,5},{5,4},{6,7},{7,6},{8,9},{9,8},{10,11... | collective-permute-start | bytes 73736 | tf_op jit(solution)/shard_map/ppermute | solution.py:496
  5.4 3.0 %collective-permute-start.1 = (bf16[48,256]{1,0:T(8,128)(2,1)S(1)}, bf16[48,256]{1,0:T(8,128)(2,1)S(1)}, u32[]{:S(2)}, u32[]{:S(2)}) collective-permute-start(bf16[48,256]{1,0:T(8,128)(2,1)S(1)} %bitcast.26), channel_id=1, source_target_pairs={{1,2},{2,1},{3,4},{4,3},{5,6},{6,5},{9,10},{10,9},{11,12},{12,11},... | collective-permute-start | bytes 73736 | tf_op jit(solution)/shard_map/ppermute | solution.py:499
  59.8 3.8 %collective-permute-start.4 = (bf16[2048,128]{1,0:T(8,128)(2,1)S(1)}, bf16[2048,128]{1,0:T(8,128)(2,1)S(1)}, u32[]{:S(2)}, u32[]{:S(2)}) collective-permute-start(bf16[2048,128]{1,0:T(8,128)(2,1)S(1)} %get-tuple-element.74), channel_id=1, source_target_pairs={{0,8},{8,0},{16,24},{24,16},{32,40},{40,32},{48,56},{56,48},{64,72... | collective-permute-start | bytes 1572872 | tf_op jit(solution)/shard_map/ppermute | solution.py:601
  64.6 32.4 %all-to-all-start.2 = ((bf16[256,8,128]{2,1,0:T(8,128)(2,1)}), bf16[256,8,128]{2,1,0:T(8,128)(2,1)S(1)}, u32[]{:S(2)}, u32[]{:S(2)}) async-start(bf16[256,8,128]{2,1,0:T(8,128)(2,1)} %bitcast.17), calls=%async_computation.2 | async-start | bytes 1048576 | tf_op jit(solution)/shard_map/all_to_all | solution.py:622
  78.2 8.7 %collective-permute-start.2 = (bf16[48,512]{1,0:T(8,128)(2,1)S(1)}, bf16[48,512]{1,0:T(8,128)(2,1)S(1)}, u32[]{:S(2)}, u32[]{:S(2)}) collective-permute-start(bf16[48,512]{1,0:T(8,128)(2,1)S(1)} %get-tuple-element.66), channel_id=1, source_target_pairs={{0,1},{1,2},{2,3},{3,4},{4,5},{5,6},{6,7},{8,9},{9,10},{10,11},{11... | collective-permute-start | bytes 147464 | tf_op jit(solution)/shard_map/ppermute | solution.py:603
  79.8 9.7 %collective-permute-start.3 = (bf16[48,512]{1,0:T(8,128)(2,1)S(1)}, bf16[48,512]{1,0:T(8,128)(2,1)S(1)}, u32[]{:S(2)}, u32[]{:S(2)}) collective-permute-start(bf16[48,512]{1,0:T(8,128)(2,1)S(1)} %get-tuple-element.67), channel_id=1, source_target_pairs={{1,0},{2,1},{3,2},{4,3},{5,4},{6,5},{7,6},{9,8},{10,9},{11,10},{12... | collective-permute-start | bytes 147464 | tf_op jit(solution)/shard_map/ppermute | solution.py:602

commit v5 on v4

--- a/solution.py
+++ b/solution.py
@@ -30,6 +30,16 @@
 
 def zero_one(condition):
     return jnp.where(condition, 1.0, 0.0).astype(BF)
+
+
+def take_shards(rows, even_out, odd_out):
+    for row in range(8):
+        for z in range(8):
+            for core, out in ((0, even_out), (1, odd_out)):
+                first = 8 * (8 * (2 * z + core) + row)
+                pair = [rows[first : first + 8], rows[1024 + first : 1024 + first + 8]]
+                at = 16 * (8 * row + z)
+                out[at : at + 16] = jnp.concatenate(pair, axis=0).astype(BF)
 
 
 def head_block():
@@ -217,7 +227,9 @@
     place_out[...] = rows[...].astype(BF)
 
 
-def coarse(place, gain, attend, scale, output, grad_out, back_out, rows, back_rows):
+def coarse(
+    place, gain, attend, scale, output, even_out, odd_out, back_out, rows, back_rows
+):
     rows[:512] = place[...].astype(F32)
     both = rows_to_lanes(rows, 0, 64, 8)
     merged, target = both[:, :512], both[:, 512:].astype(BF)
@@ -252,7 +264,7 @@
     grad = mm_tn(attn, target)
     for part in range(4):
         rows[pl.ds(part, 512, stride=4), :] = grad[:, 128 * part : 128 * part + 128]
-    grad_out[...] = rows[...].astype(BF)
+    take_shards(rows, even_out, odd_out)
     ct_triple = jnp.concatenate(
         [
             unit_back(query_raw, ct_query * lanes, block).astype(BF),
@@ -270,7 +282,8 @@
 def fine_backward(
     core,
     back,
-    grad_three,
+    even_three,
+    odd_three,
     normed,
     raw_query,
     raw_key,
@@ -293,6 +306,8 @@
     ct_key_out,
     ct_value_out,
     rows,
+    even,
+    odd,
 ):
     block = head_block()
     rows[:256] = back[...].astype(F32)
@@ -341,18 +356,15 @@
         for at, grad in enumerate(grads):
             rows[pl.ds(2 * at + half, 256, stride=6), :] = grad[:, lanes]
         rows[pl.ds(1536 + half, 256, stride=2), :] = last[:, lanes]
+    take_shards(rows, even, odd)
     own_even = core[0] == 0
-    for pair in range(16):
-        even = rows[128 * pair : 128 * pair + 64].astype(BF)
-        odd = rows[128 * pair + 64 : 128 * pair + 128].astype(BF)
-        at = 64 * pair
-        keep_out[at : at + 64] = jnp.where(own_even, even, odd)
-        send_out[at : at + 64] = jnp.where(own_even, odd, even)
-        even = grad_three[128 * pair : 128 * pair + 64]
-        odd = grad_three[128 * pair + 64 : 128 * pair + 128]
-        at = 1024 + 64 * pair
-        keep_out[at : at + 64] = jnp.where(own_even, even, odd)
-        send_out[at : at + 64] = jnp.where(own_even, odd, even)
+    for unit_at in range(64):
+        part = slice(16 * unit_at, 16 * unit_at + 16)
+        at = 32 * unit_at
+        for first, second in ((even[part], odd[part]), (even_three[part], odd_three[part])):
+            keep_out[at : at + 16] = jnp.where(own_even, first, second)
+            send_out[at : at + 16] = jnp.where(own_even, second, first)
+            at += 16
 
 
 def fine_finish(
@@ -558,9 +570,9 @@
         scratch=[pltpu.VMEM((512, 128), F32)],
     )
     place = lax.all_to_all(place.reshape(64, 8, 128), "frames", 0, 0, tiled=True)
-    grad_three, back = call(
+    even_three, odd_three, back = call(
         coarse,
-        [near((2048, 128)), jax.ShapeDtypeStruct((256, 128), BF)],
+        [near((1024, 128)), near((1024, 128)), jax.ShapeDtypeStruct((256, 128), BF)],
         place.reshape(512, 128),
         *three,
         scratch=[pltpu.VMEM((2048, 128), F32), pltpu.VMEM((256, 128), F32)],
@@ -580,7 +592,8 @@
         ],
         core,
         back.reshape(256, 128),
-        grad_three,
+        even_three,
+        odd_three,
         normed,
         raw_query,
         raw_key,
@@ -595,7 +608,7 @@
         output_two,
         merge_weight,
         smem=1,
-        scratch=[pltpu.VMEM((2048, 128), F32)],
+        scratch=[pltpu.VMEM((2048, 128), F32)] + [pltpu.VMEM((1024, 128), BF)] * 2,
     )
     pairs = [(i, i ^ 1) for i in range(lax.axis_size("frames"))]
     sent = lax.ppermute(sent, "frames", pairs)
@@ -618,7 +631,15 @@
     )
     (shares,) = call(add_pair, [jax.ShapeDtypeStruct((2048, 128), BF)], kept, sent)
     every = lax.axis_size("frames") * count
-    groups = [[at for at in range(every) if at // count % 2 == own] for own in (0, 1)]
+    groups = [
+        [
+            (16 * y_hi + 2 * z + own) * count + row
+            for row in range(count)
+            for z in range(8)
+            for y_hi in range(4)
+        ]
+        for own in (0, 1)
+    ]
     shares = lax.all_to_all(
         shares.reshape(every // 2, 8, 128),
         ("frames", "rows"),

time: 99 us -> 99.2 us (level)
  no operation moved by 1% of the time
where the time goes in v5:
time: 99.2 us; the launch traced here: 97.9 us
  blocking collectives  44.8 us (45%)
  starting transfers between devices  23.6 us (24%)
  waiting for transfers between devices  16.3 us (16%)
  Pallas kernels  11.6 us (12%)
    all_to_all x1, blocking collectives, body(): lax.all_to_all(place.reshape(64, 8, 128), 'frames', 0, 0, tiled=True)  28.6 us
    all_to_all x1, blocking collectives, body(): back = lax.all_to_all(back.reshape(64, 4, 128), 'frames', 0, 0, tiled=True)  16.2 us
    all_to_all x1, starting transfers between devices, body(): lax.all_to_all(shares.reshape(every // 2, 8, 128), ('frames', 'rows'), 0,...  13.6 us
    pallas_call x6, Pallas kernels, call(): pl.pallas_call(kernel, out_shape=outs, in_specs=[scalar] * smem + [local]...  9.33 us
    ppermute x1, waiting for transfers between devices, body(): from_above = lax.ppermute(down, 'rows', to_next)  6.79 us
    all_to_all x1, waiting for transfers between devices, body(): lax.all_to_all(shares.reshape(every // 2, 8, 128), ('frames', 'rows'), 0,...  6.14 us
    ppermute x1, starting transfers between devices, body(): lax.ppermute(jnp.where(is_even, bottom, top), 'rows', [(at, at ^ 1) for a...  4.02 us
    ppermute x1, starting transfers between devices, body(): sent = lax.ppermute(sent, 'frames', pairs)  2.31 us
  transfers between devices with their start and end apart: 6, of which 4 were waited for; matrix products, arithmetic and copies ran while one was open for 0% of the time, Pallas kernels for 4%

profile of v5, /device:TPU:1, one launch (start us, length us, event | category | flops | bytes accessed | tf_op | source)
XLA Modules:
  0.0 97.9 jit_solution(5493161540730366949)
XLA Ops:
  0.6 0.8 broadcast_select_fusion
  1.4 4.0 %collective-permute-start = (bf16[48,256]{1,0:T(8,128)(2,1)S(1)}, bf16[48,256]{1,0:T(8,128)(2,1)S(1)}, u32[]{:S(2)}, u32[]{:S(2)}) collective-permute-start(bf16[48,256]{1,0:T(8,128)(2,1)S(1)} %bitcast.27), channel_id=1, source_target_pairs={{0,1},{1,0},{2,3},{3,2},{4,5},{5,4},{6,7},{7,6},{8,9},{9,8},{10,11... | collective-permute-start | bytes 73736 | tf_op jit(solution)/shard_map/ppermute | solution.py:508
  5.4 0.7 collective-permute-start.1
  6.1 2.3 %shard_map.131 = (bf16[256,256]{1,0:T(8,128)(2,1)S(1)}, f32[1,256]{1,0:T(1,128)S(1)}, bf16[256,768]{1,0:T(8,128)(2,1)S(1)}, f32[1,4]{1,0:T(1,128)S(1)}, s32[16,1...) custom-call(bf16[256,256]{1,0:T(8,128)(2,1)} %bitcast.24, ...), custom_call_target="tpu_custom_call" | custom-call | flops 170000000 | bytes 5000000 | tf_op jit(solution)/shard_map/pallas_call | solution.py:476
  8.4 0.0 collective-permute-done.first
  8.4 0.0 collective-permute-done.1.second
  8.4 1.6 %shard_map.132 = (bf16[96,256]{1,0:T(8,128)(2,1)S(1)}, bf16[96,256]{1,0:T(8,128)(2,1)S(1)}, bf16[384,256]{1,0:T(8,128)(2,1)S(1)}, bf16[384,256]{1,0:T(8,128)(2,1...) custom-call(s32[1]{0:T(128)} %bitcast.1.rank, s32[1]{0:T(128)} %bitcast.core, ...), custom_call_target="tpu_custom_call" | custom-call | tf_op jit(solution)/shard_map/pallas_call | solution.py:448
  10.1 28.6 %all_to_all.15 = bf16[64,8,128]{2,1,0:T(8,128)(2,1)S(1)} all-to-all(bf16[64,8,128]{2,1,0:T(8,128)(2,1)S(1)} %bitcast.22), channel_id=1, replica_groups=mesh['frames'=64,'rows'=8] {'frames'}, dimensions={0} | all-to-all | bytes 262144 | tf_op jit(solution)/shard_map/all_to_all | solution.py:572
  38.7 2.6 %shard_map.133 = (bf16[1024,128]{1,0:T(8,128)(2,1)S(1)}, bf16[1024,128]{1,0:T(8,128)(2,1)S(1)}, bf16[256,128]{1,0:T(8,128)(2,1)S(1)}) custom-call(bf16[512,128]{1,0:T(8,128)(2,1)S(1)} %bitcast.20, f32[1,512]{1,0:T(1,128)S(1)} %get-tuple-element.51.gain, bf16[512,1536]{1,0:T(8,128)(2,1)S(1)} %get-tuple-element.52.attend, f32[1,8]{1,0:T(1,128)S(1)} %get-tuple-element.53.scale, ...), custom_call_target="tpu_custom_call" | custom-call | tf_op jit(solution)/shard_map/pallas_call | solution.py:448
  41.3 16.2 %all_to_all.16 = bf16[64,4,128]{2,1,0:T(4,128)(2,1)S(1)} all-to-all(bf16[64,4,128]{2,1,0:T(4,128)(2,1)S(1)} %bitcast.23), channel_id=1, replica_groups=mesh['frames'=64,'rows'=8] {'frames'}, dimensions={0} | all-to-all | bytes 131072 | tf_op jit(solution)/shard_map/all_to_all | solution.py:580
  57.5 2.3 %shard_map.134 = (bf16[2048,128]{1,0:T(8,128)(2,1)S(1)}, bf16[2048,128]{1,0:T(8,128)(2,1)S(1)}, bf16[48,512]{1,0:T(8,128)(2,1)S(1)}, bf16[48,512]{1,0:T(8,128)(2...) custom-call(s32[1]{0:T(128)} %bitcast.core, ...), custom_call_target="tpu_custom_call" | custom-call | tf_op jit(solution)/shard_map/pallas_call | solution.py:448
  59.9 2.3 %collective-permute-start.4 = (bf16[2048,128]{1,0:T(8,128)(2,1)S(1)}, bf16[2048,128]{1,0:T(8,128)(2,1)S(1)}, u32[]{:S(2)}, u32[]{:S(2)}) collective-permute-start(bf16[2048,128]{1,0:T(8,128)(2,1)S(1)} %get-tuple-element.76), channel_id=1, source_target_pairs={{0,8},{8,0},{16,24},{24,16},{32,40},{40,32},{48,56},{56,48},{64,72... | collective-permute-start | bytes 1572872 | tf_op jit(solution)/shard_map/ppermute | solution.py:614
  62.2 1.5 %collective-permute-done.4.sent = bf16[2048,128]{1,0:T(8,128)(2,1)S(1)} collective-permute-done((bf16[2048,128]{1,0:T(8,128)(2,1)S(1)}, bf16[2048,128]{1,0:T(8,128)(2,1)S(1)}, u32[]{:S(2)}, u32[]{:S(2)}) %collective-permute-start.4) | collective-permute-done | bytes 524320 | tf_op jit(solution)/shard_map/ppermute | solution.py:614
  63.7 0.9 shard_map.136
  64.6 13.6 %all-to-all-start.2 = ((bf16[256,8,128]{2,1,0:T(8,128)(2,1)}), bf16[256,8,128]{2,1,0:T(8,128)(2,1)S(1)}, u32[]{:S(2)}, u32[]{:S(2)}) async-start(bf16[256,8,128]{2,1,0:T(8,128)(2,1)} %bitcast.17), calls=%async_computation.2 | async-start | bytes 1048576 | tf_op jit(solution)/shard_map/all_to_all | solution.py:643
  78.3 1.7 %collective-permute-start.2 = (bf16[48,512]{1,0:T(8,128)(2,1)S(1)}, bf16[48,512]{1,0:T(8,128)(2,1)S(1)}, u32[]{:S(2)}, u32[]{:S(2)}) collective-permute-start(bf16[48,512]{1,0:T(8,128)(2,1)S(1)} %get-tuple-element.68), channel_id=1, source_target_pairs={{0,1},{1,2},{2,3},{3,4},{4,5},{5,6},{6,7},{8,9},{9,10},{10,11},{11... | collective-permute-start | bytes 147464 | tf_op jit(solution)/shard_map/ppermute | solution.py:616
  80.0 1.3 %collective-permute-start.3 = (bf16[48,512]{1,0:T(8,128)(2,1)S(1)}, bf16[48,512]{1,0:T(8,128)(2,1)S(1)}, u32[]{:S(2)}, u32[]{:S(2)}) collective-permute-start(bf16[48,512]{1,0:T(8,128)(2,1)S(1)} %get-tuple-element.69), channel_id=1, source_target_pairs={{1,0},{2,1},{3,2},{4,3},{5,4},{6,5},{7,6},{9,8},{10,9},{11,10},{12... | collective-permute-start | bytes 147464 | tf_op jit(solution)/shard_map/ppermute | solution.py:615
  81.3 6.8 %collective-permute-done.2.from_above = bf16[48,512]{1,0:T(8,128)(2,1)S(1)} collective-permute-done((bf16[48,512]{1,0:T(8,128)(2,1)S(1)}, bf16[48,512]{1,0:T(8,128)(2,1)S(1)}, u32[]{:S(2)}, u32[]{:S(2)}) %collective-permute-start.2) | collective-permute-done | bytes 49184 | tf_op jit(solution)/shard_map/ppermute | solution.py:616
  88.0 1.9 %collective-permute-done.3.from_below = bf16[48,512]{1,0:T(8,128)(2,1)S(1)} collective-permute-done((bf16[48,512]{1,0:T(8,128)(2,1)S(1)}, bf16[48,512]{1,0:T(8,128)(2,1)S(1)}, u32[]{:S(2)}, u32[]{:S(2)}) %collective-permute-start.3) | collective-permute-done | bytes 49184 | tf_op jit(solution)/shard_map/ppermute | solution.py:615
  89.9 1.2 %shard_map.135 = (bf16[256,256]{1,0:T(8,128)(2,1)}, f32[8,128]{1,0:T(8,128)S(1)}) custom-call(bf16[48,512]{1,0:T(8,128)(2,1)S(1)} %collective-permute-done.2.from_above, bf16[48,512]{1,0:T(8,128)(2,1)S(1)} %collective-permute-done.3.from_below, bf16[256,256]{1,0:T(8,128)(2,1)S(1)} %get-tuple-element.70.ct_query, ...), custom_call_target="tpu_custom_call" | custom-call | flops 170000000 | bytes 2000000 | tf_op jit(solution)/shard_map/pallas_call | solution.py:448
  91.1 6.1 %all-to-all-done.2.shares = bf16[256,8,128]{2,1,0:T(8,128)(2,1)S(1)} async-done(((bf16[256,8,128]{2,1,0:T(8,128)(2,1)}), bf16[256,8,128]{2,1,0:T(8,128)(2,1)S(1)}, u32[]{:S(2)}, u32[]{:S(2)}) %all-to-all-start.2) | async-done | bytes 524320 | tf_op jit(solution)/shard_map/all_to_all | solution.py:643
  97.2 0.7 shard_map.137
Async XLA Ops:
  1.4 7.0 %collective-permute-start = (bf16[48,256]{1,0:T(8,128)(2,1)S(1)}, bf16[48,256]{1,0:T(8,128)(2,1)S(1)}, u32[]{:S(2)}, u32[]{:S(2)}) collective-permute-start(bf16[48,256]{1,0:T(8,128)(2,1)S(1)} %bitcast.27), channel_id=1, source_target_pairs={{0,1},{1,0},{2,3},{3,2},{4,5},{5,4},{6,7},{7,6},{8,9},{9,8},{10,11... | collective-permute-start | bytes 73736 | tf_op jit(solution)/shard_map/ppermute | solution.py:508
  5.4 3.0 %collective-permute-start.1 = (bf16[48,256]{1,0:T(8,128)(2,1)S(1)}, bf16[48,256]{1,0:T(8,128)(2,1)S(1)}, u32[]{:S(2)}, u32[]{:S(2)}) collective-permute-start(bf16[48,256]{1,0:T(8,128)(2,1)S(1)} %bitcast.26), channel_id=1, source_target_pairs={{1,2},{2,1},{3,4},{4,3},{5,6},{6,5},{9,10},{10,9},{11,12},{12,11},... | collective-permute-start | bytes 73736 | tf_op jit(solution)/shard_map/ppermute | solution.py:511
  59.9 3.8 %collective-permute-start.4 = (bf16[2048,128]{1,0:T(8,128)(2,1)S(1)}, bf16[2048,128]{1,0:T(8,128)(2,1)S(1)}, u32[]{:S(2)}, u32[]{:S(2)}) collective-permute-start(bf16[2048,128]{1,0:T(8,128)(2,1)S(1)} %get-tuple-element.76), channel_id=1, source_target_pairs={{0,8},{8,0},{16,24},{24,16},{32,40},{40,32},{48,56},{56,48},{64,72... | collective-permute-start | bytes 1572872 | tf_op jit(solution)/shard_map/ppermute | solution.py:614
  64.6 32.6 %all-to-all-start.2 = ((bf16[256,8,128]{2,1,0:T(8,128)(2,1)}), bf16[256,8,128]{2,1,0:T(8,128)(2,1)S(1)}, u32[]{:S(2)}, u32[]{:S(2)}) async-start(bf16[256,8,128]{2,1,0:T(8,128)(2,1)} %bitcast.17), calls=%async_computation.2 | async-start | bytes 1048576 | tf_op jit(solution)/shard_map/all_to_all | solution.py:643
  78.3 9.8 %collective-permute-start.2 = (bf16[48,512]{1,0:T(8,128)(2,1)S(1)}, bf16[48,512]{1,0:T(8,128)(2,1)S(1)}, u32[]{:S(2)}, u32[]{:S(2)}) collective-permute-start(bf16[48,512]{1,0:T(8,128)(2,1)S(1)} %get-tuple-element.68), channel_id=1, source_target_pairs={{0,1},{1,2},{2,3},{3,4},{4,5},{5,6},{6,7},{8,9},{9,10},{10,11},{11... | collective-permute-start | bytes 147464 | tf_op jit(solution)/shard_map/ppermute | solution.py:616
  80.0 10.0 %collective-permute-start.3 = (bf16[48,512]{1,0:T(8,128)(2,1)S(1)}, bf16[48,512]{1,0:T(8,128)(2,1)S(1)}, u32[]{:S(2)}, u32[]{:S(2)}) collective-permute-start(bf16[48,512]{1,0:T(8,128)(2,1)S(1)} %get-tuple-element.69), channel_id=1, source_target_pairs={{1,0},{2,1},{3,2},{4,3},{5,4},{6,5},{7,6},{9,8},{10,9},{11,10},{12... | collective-permute-start | bytes 147464 | tf_op jit(solution)/shard_map/ppermute | solution.py:615

commit v6 on v4

--- a/solution.py
+++ b/solution.py
@@ -9,6 +9,7 @@
 BF = jnp.bfloat16
 F32 = jnp.float32
 HALO = 48
+SPARE = 16
 VMEM_BYTES = 32 * 1024 * 1024
 
 
@@ -157,8 +158,8 @@
 def fine_forward(
     rank,
     core,
-    first,
-    second,
+    far,
+    near_by,
     query,
     own_keys,
     own_value,
@@ -180,8 +181,8 @@
 ):
     del core
     is_even = (rank[0] & 1) == 0
-    above = jnp.where(is_even, second[...].astype(F32), first[...].astype(F32))
-    below = jnp.where(is_even, first[...].astype(F32), second[...].astype(F32))
+    above = jnp.where(is_even, far[...].astype(F32), near_by[...].astype(F32))
+    below = jnp.where(is_even, near_by[...].astype(F32), far[...].astype(F32))
     halo = jnp.concatenate([above, below], axis=0)
     normed = rms(halo, gain[...])
     beside_out[...] = normed
@@ -214,7 +215,7 @@
     for group in range(1, 4):
         merged += mm(patches[64 * group : 64 * group + 64], merge[256 * group : 256 * group + 256])
     lanes_to_rows(jnp.concatenate([merged, cotangent[...].astype(F32)], axis=1), rows, 0)
-    place_out[...] = rows[...].astype(BF)
+    place_out[...] = rows[:512].astype(BF)
 
 
 def coarse(place, gain, attend, scale, output, grad_out, back_out, rows, back_rows):
@@ -252,7 +253,7 @@
     grad = mm_tn(attn, target)
     for part in range(4):
         rows[pl.ds(part, 512, stride=4), :] = grad[:, 128 * part : 128 * part + 128]
-    grad_out[...] = rows[...].astype(BF)
+    grad_out[...] = rows[:2048].astype(BF)
     ct_triple = jnp.concatenate(
         [
             unit_back(query_raw, ct_query * lanes, block).astype(BF),
@@ -264,7 +265,7 @@
     ct_normed = mm_nt(ct_triple, attend[...]).astype(BF).astype(F32)
     ct_merged = target.astype(F32) + rms_back(merged, gain[...], ct_normed)
     lanes_to_rows(ct_merged, back_rows, 0)
-    back_out[...] = back_rows[...].astype(BF)
+    back_out[...] = back_rows[:256].astype(BF)
 
 
 def fine_backward(
@@ -490,15 +491,12 @@
     to_next = [(i, i + 1) for i in range(count - 1)]
     to_last = [(i + 1, i) for i in range(count - 1)]
     own = tokens.reshape(256, 256)
-    place = lax.axis_index("rows")
-    is_even = (place & 1) == 0
+    is_even = (lax.axis_index("rows") & 1) == 0
     top, bottom = own[:HALO], own[256 - HALO :]
-    first = lax.ppermute(
-        jnp.where(is_even, bottom, top), "rows", [(at, at ^ 1) for at in range(count)]
-    )
-    second = lax.ppermute(
-        jnp.where(is_even, top, bottom), "rows", [(at, ((at + 1) ^ 1) - 1) for at in range(1, count - 1)]
-    )
+    pairs = [(at, ((at + 1) ^ 1) - 1) for at in range(1, count - 1)]
+    far = lax.ppermute(jnp.where(is_even, top, bottom), "rows", pairs)
+    pairs = [(at, at ^ 1) for at in range(count)]
+    near_by = lax.ppermute(jnp.where(is_even, bottom, top), "rows", pairs)
     rank = lax.axis_index("rows").astype(jnp.int32).reshape(1)
     core = (lax.axis_index("frames") & 1).astype(jnp.int32).reshape(1)
     square = (256, 256)
@@ -542,8 +540,8 @@
         ],
         rank,
         core,
-        first,
-        second,
+        far,
+        near_by,
         query,
         own_keys,
         own_value,
@@ -555,7 +553,7 @@
         cot,
         merge_weight,
         smem=2,
-        scratch=[pltpu.VMEM((512, 128), F32)],
+        scratch=[pltpu.VMEM((512 + SPARE, 128), F32)],
     )
     place = lax.all_to_all(place.reshape(64, 8, 128), "frames", 0, 0, tiled=True)
     grad_three, back = call(
@@ -563,7 +561,7 @@
         [near((2048, 128)), jax.ShapeDtypeStruct((256, 128), BF)],
         place.reshape(512, 128),
         *three,
-        scratch=[pltpu.VMEM((2048, 128), F32), pltpu.VMEM((256, 128), F32)],
+        scratch=[pltpu.VMEM((2048 + SPARE, 128), F32), pltpu.VMEM((256 + SPARE, 128), F32)],
     )
     back = lax.all_to_all(back.reshape(64, 4, 128), "frames", 0, 0, tiled=True)
     kept, sent, up, down, ct_mixed, ct_query, ct_key, ct_value = call(
@@ -595,7 +593,7 @@
         output_two,
         merge_weight,
         smem=1,
-        scratch=[pltpu.VMEM((2048, 128), F32)],
+        scratch=[pltpu.VMEM((2048 + SPARE, 128), F32)],
     )
     pairs = [(i, i ^ 1) for i in range(lax.axis_size("frames"))]
     sent = lax.ppermute(sent, "frames", pairs)

time: 99 us -> 98.6 us (level)
  starting transfers between devices: 23.5 us -> 21.5 us
  blocking collectives: 44.8 us -> 46.5 us
    all_to_all x1, starting transfers between devices: 13.6 us -> 9.31 us  [body(): lax.all_to_all(shares.reshape(every // 2, 8, 128), ('frames', 'rows'), 0,...]
    ppermute x2, starting transfers between devices: 4.68 us -> 7.03 us  [the longest x1 6.38 us: body(): near_by = lax.ppermute(jnp.where(is_even, bottom, top), 'rows', pairs)]
    all_to_all x1, blocking collectives: 28.6 us -> 29.7 us  [body(): lax.all_to_all(place.reshape(64, 8, 128), 'frames', 0, 0, tiled=True)]
where the time goes in v6:
time: 98.6 us; the launch traced here: 97.3 us
  blocking collectives  46.5 us (47%)
  starting transfers between devices  21.5 us (22%)
  waiting for transfers between devices  16.2 us (16%)
  Pallas kernels  11.6 us (12%)
    all_to_all x1, blocking collectives, body(): lax.all_to_all(place.reshape(64, 8, 128), 'frames', 0, 0, tiled=True)  29.7 us
    all_to_all x1, blocking collectives, body(): back = lax.all_to_all(back.reshape(64, 4, 128), 'frames', 0, 0, tiled=True)  16.8 us
    all_to_all x1, starting transfers between devices, body(): lax.all_to_all(shares.reshape(every // 2, 8, 128), ('frames', 'rows'), 0,...  9.31 us
    pallas_call x6, Pallas kernels, call(): pl.pallas_call(kernel, out_shape=outs, in_specs=[scalar] * smem + [local]...  9.26 us
    ppermute x1, starting transfers between devices, body(): near_by = lax.ppermute(jnp.where(is_even, bottom, top), 'rows', pairs)  6.38 us
    all_to_all x1, waiting for transfers between devices, body(): lax.all_to_all(shares.reshape(every // 2, 8, 128), ('frames', 'rows'), 0,...  6.22 us
    ppermute x1, waiting for transfers between devices, body(): from_above = lax.ppermute(down, 'rows', to_next)  5.81 us
    ppermute x1, waiting for transfers between devices, body(): from_below = lax.ppermute(up, 'rows', to_last)  2.62 us
  transfers between devices with their start and end apart: 6, of which 4 were waited for; matrix products, arithmetic and copies ran while one was open for 0% of the time, Pallas kernels for 4%

profile of v6, /device:TPU:1, one launch (start us, length us, event | category | flops | bytes accessed | tf_op | source)
XLA Modules:
  0.0 97.3 jit_solution(4055804524564649541)
XLA Ops:
  0.6 0.8 broadcast_select_fusion
  1.4 0.7 collective-permute-start
  2.1 6.4 %collective-permute-start.1 = (bf16[48,256]{1,0:T(8,128)(2,1)S(1)}, bf16[48,256]{1,0:T(8,128)(2,1)S(1)}, u32[]{:S(2)}, u32[]{:S(2)}) collective-permute-start(bf16[48,256]{1,0:T(8,128)(2,1)S(1)} %bitcast.26), channel_id=1, source_target_pairs={{0,1},{1,0},{2,3},{3,2},{4,5},{5,4},{6,7},{7,6},{8,9},{9,8},{10,11... | collective-permute-start | bytes 73736 | tf_op jit(solution)/shard_map/ppermute | solution.py:499
  8.4 2.3 %shard_map.131 = (bf16[256,256]{1,0:T(8,128)(2,1)S(1)}, f32[1,256]{1,0:T(1,128)S(1)}, bf16[256,768]{1,0:T(8,128)(2,1)S(1)}, f32[1,4]{1,0:T(1,128)S(1)}, s32[16,1...) custom-call(bf16[256,256]{1,0:T(8,128)(2,1)} %bitcast.24, ...), custom_call_target="tpu_custom_call" | custom-call | flops 170000000 | bytes 5000000 | tf_op jit(solution)/shard_map/pallas_call | solution.py:465
  10.8 0.0 collective-permute-done.far
  10.8 0.0 collective-permute-done.1.near_by
  10.8 1.6 %shard_map.132 = (bf16[96,256]{1,0:T(8,128)(2,1)S(1)}, bf16[96,256]{1,0:T(8,128)(2,1)S(1)}, bf16[384,256]{1,0:T(8,128)(2,1)S(1)}, bf16[384,256]{1,0:T(8,128)(2,1...) custom-call(s32[1]{0:T(128)} %bitcast.1.rank, s32[1]{0:T(128)} %bitcast.core, ...), custom_call_target="tpu_custom_call" | custom-call | tf_op jit(solution)/shard_map/pallas_call | solution.py:437
  12.4 29.7 %all_to_all.15 = bf16[64,8,128]{2,1,0:T(8,128)(2,1)S(1)} all-to-all(bf16[64,8,128]{2,1,0:T(8,128)(2,1)S(1)} %bitcast.22), channel_id=1, replica_groups=mesh['frames'=64,'rows'=8] {'frames'}, dimensions={0} | all-to-all | bytes 262144 | tf_op jit(solution)/shard_map/all_to_all | solution.py:558
  42.1 2.6 %shard_map.133 = (bf16[2048,128]{1,0:T(8,128)(2,1)S(1)}, bf16[256,128]{1,0:T(8,128)(2,1)S(1)}) custom-call(bf16[512,128]{1,0:T(8,128)(2,1)S(1)} %bitcast.20, f32[1,512]{1,0:T(1,128)S(1)} %get-tuple-element.50.gain, bf16[512,1536]{1,0:T(8,128)(2,1)S(1)} %get-tuple-element.51.attend, f32[1,8]{1,0:T(1,128)S(1)} %get-tuple-element.52.scale, ...), custom_call_target="tpu_custom_call" | custom-call | tf_op jit(solution)/shard_map/pallas_call | solution.py:437
  44.7 16.8 %all_to_all.16 = bf16[64,4,128]{2,1,0:T(4,128)(2,1)S(1)} all-to-all(bf16[64,4,128]{2,1,0:T(4,128)(2,1)S(1)} %bitcast.23), channel_id=1, replica_groups=mesh['frames'=64,'rows'=8] {'frames'}, dimensions={0} | all-to-all | bytes 131072 | tf_op jit(solution)/shard_map/all_to_all | solution.py:566
  61.5 2.2 %shard_map.134 = (bf16[2048,128]{1,0:T(8,128)(2,1)S(1)}, bf16[2048,128]{1,0:T(8,128)(2,1)S(1)}, bf16[48,512]{1,0:T(8,128)(2,1)S(1)}, bf16[48,512]{1,0:T(8,128)(2...) custom-call(s32[1]{0:T(128)} %bitcast.core, ...), custom_call_target="tpu_custom_call" | custom-call | tf_op jit(solution)/shard_map/pallas_call | solution.py:437
  63.8 2.3 %collective-permute-start.4 = (bf16[2048,128]{1,0:T(8,128)(2,1)S(1)}, bf16[2048,128]{1,0:T(8,128)(2,1)S(1)}, u32[]{:S(2)}, u32[]{:S(2)}) collective-permute-start(bf16[2048,128]{1,0:T(8,128)(2,1)S(1)} %get-tuple-element.74), channel_id=1, source_target_pairs={{0,8},{8,0},{16,24},{24,16},{32,40},{40,32},{48,56},{56,48},{64,72... | collective-permute-start | bytes 1572872 | tf_op jit(solution)/shard_map/ppermute | solution.py:599
  66.1 1.5 %collective-permute-done.4.sent = bf16[2048,128]{1,0:T(8,128)(2,1)S(1)} collective-permute-done((bf16[2048,128]{1,0:T(8,128)(2,1)S(1)}, bf16[2048,128]{1,0:T(8,128)(2,1)S(1)}, u32[]{:S(2)}, u32[]{:S(2)}) %collective-permute-start.4) | collective-permute-done | bytes 524320 | tf_op jit(solution)/shard_map/ppermute | solution.py:599
  67.6 0.9 shard_map.136
  68.5 9.3 %all-to-all-start.2 = ((bf16[256,8,128]{2,1,0:T(8,128)(2,1)}), bf16[256,8,128]{2,1,0:T(8,128)(2,1)S(1)}, u32[]{:S(2)}, u32[]{:S(2)}) async-start(bf16[256,8,128]{2,1,0:T(8,128)(2,1)} %bitcast.17), calls=%async_computation.2 | async-start | bytes 1048576 | tf_op jit(solution)/shard_map/all_to_all | solution.py:620
  77.9 1.6 %collective-permute-start.2 = (bf16[48,512]{1,0:T(8,128)(2,1)S(1)}, bf16[48,512]{1,0:T(8,128)(2,1)S(1)}, u32[]{:S(2)}, u32[]{:S(2)}) collective-permute-start(bf16[48,512]{1,0:T(8,128)(2,1)S(1)} %get-tuple-element.66), channel_id=1, source_target_pairs={{0,1},{1,2},{2,3},{3,4},{4,5},{5,6},{6,7},{8,9},{9,10},{10,11},{11... | collective-permute-start | bytes 147464 | tf_op jit(solution)/shard_map/ppermute | solution.py:601
  79.5 1.3 %collective-permute-start.3 = (bf16[48,512]{1,0:T(8,128)(2,1)S(1)}, bf16[48,512]{1,0:T(8,128)(2,1)S(1)}, u32[]{:S(2)}, u32[]{:S(2)}) collective-permute-start(bf16[48,512]{1,0:T(8,128)(2,1)S(1)} %get-tuple-element.67), channel_id=1, source_target_pairs={{1,0},{2,1},{3,2},{4,3},{5,4},{6,5},{7,6},{9,8},{10,9},{11,10},{12... | collective-permute-start | bytes 147464 | tf_op jit(solution)/shard_map/ppermute | solution.py:600
  80.8 5.8 %collective-permute-done.2.from_above = bf16[48,512]{1,0:T(8,128)(2,1)S(1)} collective-permute-done((bf16[48,512]{1,0:T(8,128)(2,1)S(1)}, bf16[48,512]{1,0:T(8,128)(2,1)S(1)}, u32[]{:S(2)}, u32[]{:S(2)}) %collective-permute-start.2) | collective-permute-done | bytes 49184 | tf_op jit(solution)/shard_map/ppermute | solution.py:601
  86.6 2.6 %collective-permute-done.3.from_below = bf16[48,512]{1,0:T(8,128)(2,1)S(1)} collective-permute-done((bf16[48,512]{1,0:T(8,128)(2,1)S(1)}, bf16[48,512]{1,0:T(8,128)(2,1)S(1)}, u32[]{:S(2)}, u32[]{:S(2)}) %collective-permute-start.3) | collective-permute-done | bytes 49184 | tf_op jit(solution)/shard_map/ppermute | solution.py:600
  89.2 1.2 %shard_map.135 = (bf16[256,256]{1,0:T(8,128)(2,1)}, f32[8,128]{1,0:T(8,128)S(1)}) custom-call(bf16[48,512]{1,0:T(8,128)(2,1)S(1)} %collective-permute-done.2.from_above, bf16[48,512]{1,0:T(8,128)(2,1)S(1)} %collective-permute-done.3.from_below, bf16[256,256]{1,0:T(8,128)(2,1)S(1)} %get-tuple-element.68.ct_query, ...), custom_call_target="tpu_custom_call" | custom-call | flops 170000000 | bytes 2000000 | tf_op jit(solution)/shard_map/pallas_call | solution.py:437
  90.4 6.2 %all-to-all-done.2.shares = bf16[256,8,128]{2,1,0:T(8,128)(2,1)S(1)} async-done(((bf16[256,8,128]{2,1,0:T(8,128)(2,1)}), bf16[256,8,128]{2,1,0:T(8,128)(2,1)S(1)}, u32[]{:S(2)}, u32[]{:S(2)}) %all-to-all-start.2) | async-done | bytes 524320 | tf_op jit(solution)/shard_map/all_to_all | solution.py:620
  96.6 0.7 shard_map.137
Async XLA Ops:
  1.4 9.4 %collective-permute-start = (bf16[48,256]{1,0:T(8,128)(2,1)S(1)}, bf16[48,256]{1,0:T(8,128)(2,1)S(1)}, u32[]{:S(2)}, u32[]{:S(2)}) collective-permute-start(bf16[48,256]{1,0:T(8,128)(2,1)S(1)} %bitcast.27), channel_id=1, source_target_pairs={{1,2},{2,1},{3,4},{4,3},{5,6},{6,5},{9,10},{10,9},{11,12},{12,11},... | collective-permute-start | bytes 73736 | tf_op jit(solution)/shard_map/ppermute | solution.py:497
  2.1 8.7 %collective-permute-start.1 = (bf16[48,256]{1,0:T(8,128)(2,1)S(1)}, bf16[48,256]{1,0:T(8,128)(2,1)S(1)}, u32[]{:S(2)}, u32[]{:S(2)}) collective-permute-start(bf16[48,256]{1,0:T(8,128)(2,1)S(1)} %bitcast.26), channel_id=1, source_target_pairs={{0,1},{1,0},{2,3},{3,2},{4,5},{5,4},{6,7},{7,6},{8,9},{9,8},{10,11... | collective-permute-start | bytes 73736 | tf_op jit(solution)/shard_map/ppermute | solution.py:499
  63.8 3.8 %collective-permute-start.4 = (bf16[2048,128]{1,0:T(8,128)(2,1)S(1)}, bf16[2048,128]{1,0:T(8,128)(2,1)S(1)}, u32[]{:S(2)}, u32[]{:S(2)}) collective-permute-start(bf16[2048,128]{1,0:T(8,128)(2,1)S(1)} %get-tuple-element.74), channel_id=1, source_target_pairs={{0,8},{8,0},{16,24},{24,16},{32,40},{40,32},{48,56},{56,48},{64,72... | collective-permute-start | bytes 1572872 | tf_op jit(solution)/shard_map/ppermute | solution.py:599
  68.5 28.1 %all-to-all-start.2 = ((bf16[256,8,128]{2,1,0:T(8,128)(2,1)}), bf16[256,8,128]{2,1,0:T(8,128)(2,1)S(1)}, u32[]{:S(2)}, u32[]{:S(2)}) async-start(bf16[256,8,128]{2,1,0:T(8,128)(2,1)} %bitcast.17), calls=%async_computation.2 | async-start | bytes 1048576 | tf_op jit(solution)/shard_map/all_to_all | solution.py:620
  77.9 8.7 %collective-permute-start.2 = (bf16[48,512]{1,0:T(8,128)(2,1)S(1)}, bf16[48,512]{1,0:T(8,128)(2,1)S(1)}, u32[]{:S(2)}, u32[]{:S(2)}) collective-permute-start(bf16[48,512]{1,0:T(8,128)(2,1)S(1)} %get-tuple-element.66), channel_id=1, source_target_pairs={{0,1},{1,2},{2,3},{3,4},{4,5},{5,6},{6,7},{8,9},{9,10},{10,11},{11... | collective-permute-start | bytes 147464 | tf_op jit(solution)/shard_map/ppermute | solution.py:601
  79.5 9.7 %collective-permute-start.3 = (bf16[48,512]{1,0:T(8,128)(2,1)S(1)}, bf16[48,512]{1,0:T(8,128)(2,1)S(1)}, u32[]{:S(2)}, u32[]{:S(2)}) collective-permute-start(bf16[48,512]{1,0:T(8,128)(2,1)S(1)} %get-tuple-element.67), channel_id=1, source_target_pairs={{1,0},{2,1},{3,2},{4,3},{5,4},{6,5},{7,6},{9,8},{10,9},{11,10},{12... | collective-permute-start | bytes 147464 | tf_op jit(solution)/shard_map/ppermute | solution.py:600

commit v7 on v6

--- a/solution.py
+++ b/solution.py
@@ -393,8 +393,16 @@
     done_out[...] = jnp.zeros((8, 128), F32)
 
 
-def add_pair(kept, sent, out):
-    out[...] = (kept[...].astype(F32) + sent[...].astype(F32)).astype(BF)
+def add_pair(kept, sent, out, total, sems):
+    copies = []
+    for quarter in range(4):
+        part = pl.ds(512 * quarter, 512)
+        total[part] = (kept[part].astype(F32) + sent[part].astype(F32)).astype(BF)
+        copy = pltpu.make_async_copy(total.at[part], out.at[part], sems.at[quarter])
+        copy.start()
+        copies.append(copy)
+    for copy in copies:
+        copy.wait()
 
 
 def add_all(shares, done, out):
@@ -614,7 +622,14 @@
         attend_two,
         cost=pl.CostEstimate(flops=170_000_000, bytes_accessed=2_000_000, transcendentals=0),
     )
-    (shares,) = call(add_pair, [jax.ShapeDtypeStruct((2048, 128), BF)], kept, sent)
+    shares = pl.pallas_call(
+        add_pair,
+        out_shape=jax.ShapeDtypeStruct((2048, 128), BF),
+        in_specs=[pl.BlockSpec(memory_space=pltpu.VMEM)] * 2,
+        out_specs=pl.BlockSpec(memory_space=pltpu.HBM),
+        scratch_shapes=[pltpu.VMEM((2048, 128), BF), pltpu.SemaphoreType.DMA((4,))],
+        compiler_params=pltpu.CompilerParams(vmem_limit_bytes=VMEM_BYTES),
+    )(kept, sent)
     every = lax.axis_size("frames") * count
     groups = [[at for at in range(every) if at // count % 2 == own] for own in (0, 1)]
     shares = lax.all_to_all(

time: 98.6 us -> 98.6 us (level)
    pallas_call x6 -> x5, Pallas kernels: 9.26 us -> 8.33 us  [call(): pl.pallas_call(kernel, out_shape=outs, in_specs=[scalar] * smem + [local]...]
where the time goes in v7:
time: 98.6 us; the launch traced here: 97.2 us
  blocking collectives  46.5 us (47%)
  starting transfers between devices  21.5 us (22%)
  waiting for transfers between devices  16.2 us (16%)
  Pallas kernels  11.5 us (12%)
    all_to_all x1, blocking collectives, body(): lax.all_to_all(place.reshape(64, 8, 128), 'frames', 0, 0, tiled=True)  29.7 us
    all_to_all x1, blocking collectives, body(): back = lax.all_to_all(back.reshape(64, 4, 128), 'frames', 0, 0, tiled=True)  16.8 us
    all_to_all x1, starting transfers between devices, body(): lax.all_to_all(shares.reshape(every // 2, 8, 128), ('frames', 'rows'), 0,...  9.32 us
    pallas_call x5, Pallas kernels, call(): pl.pallas_call(kernel, out_shape=outs, in_specs=[scalar] * smem + [local]...  8.33 us
    ppermute x1, starting transfers between devices, body(): near_by = lax.ppermute(jnp.where(is_even, bottom, top), 'rows', pairs)  6.38 us
    all_to_all x1, waiting for transfers between devices, body(): lax.all_to_all(shares.reshape(every // 2, 8, 128), ('frames', 'rows'), 0,...  6.22 us
    ppermute x1, waiting for transfers between devices, body(): from_above = lax.ppermute(down, 'rows', to_next)  5.81 us
    ppermute x1, waiting for transfers between devices, body(): from_below = lax.ppermute(up, 'rows', to_last)  2.62 us
  transfers between devices with their start and end apart: 6, of which 4 were waited for; matrix products, arithmetic and copies ran while one was open for 0% of the time, Pallas kernels for 4%

profile of v7, /device:TPU:1, one launch (start us, length us, event | category | flops | bytes accessed | tf_op | source)
XLA Modules:
  0.0 97.2 jit_solution(15613045554613772681)
XLA Ops:
  0.6 0.8 broadcast_select_fusion
  1.4 0.7 collective-permute-start
  2.1 6.4 %collective-permute-start.1 = (bf16[48,256]{1,0:T(8,128)(2,1)S(1)}, bf16[48,256]{1,0:T(8,128)(2,1)S(1)}, u32[]{:S(2)}, u32[]{:S(2)}) collective-permute-start(bf16[48,256]{1,0:T(8,128)(2,1)S(1)} %bitcast.26), channel_id=1, source_target_pairs={{0,1},{1,0},{2,3},{3,2},{4,5},{5,4},{6,7},{7,6},{8,9},{9,8},{10,11... | collective-permute-start | bytes 73736 | tf_op jit(solution)/shard_map/ppermute | solution.py:507
  8.4 2.3 %shard_map.131 = (bf16[256,256]{1,0:T(8,128)(2,1)S(1)}, f32[1,256]{1,0:T(1,128)S(1)}, bf16[256,768]{1,0:T(8,128)(2,1)S(1)}, f32[1,4]{1,0:T(1,128)S(1)}, s32[16,1...) custom-call(bf16[256,256]{1,0:T(8,128)(2,1)} %bitcast.24, ...), custom_call_target="tpu_custom_call" | custom-call | flops 170000000 | bytes 5000000 | tf_op jit(solution)/shard_map/pallas_call | solution.py:473
  10.8 0.0 collective-permute-done.far
  10.8 0.0 collective-permute-done.1.near_by
  10.8 1.6 %shard_map.132 = (bf16[96,256]{1,0:T(8,128)(2,1)S(1)}, bf16[96,256]{1,0:T(8,128)(2,1)S(1)}, bf16[384,256]{1,0:T(8,128)(2,1)S(1)}, bf16[384,256]{1,0:T(8,128)(2,1...) custom-call(s32[1]{0:T(128)} %bitcast.1.rank, s32[1]{0:T(128)} %bitcast.core, ...), custom_call_target="tpu_custom_call" | custom-call | tf_op jit(solution)/shard_map/pallas_call | solution.py:445
  12.4 29.7 %all_to_all.15 = bf16[64,8,128]{2,1,0:T(8,128)(2,1)S(1)} all-to-all(bf16[64,8,128]{2,1,0:T(8,128)(2,1)S(1)} %bitcast.22), channel_id=1, replica_groups=mesh['frames'=64,'rows'=8] {'frames'}, dimensions={0} | all-to-all | bytes 262144 | tf_op jit(solution)/shard_map/all_to_all | solution.py:566
  42.1 2.6 %shard_map.133 = (bf16[2048,128]{1,0:T(8,128)(2,1)S(1)}, bf16[256,128]{1,0:T(8,128)(2,1)S(1)}) custom-call(bf16[512,128]{1,0:T(8,128)(2,1)S(1)} %bitcast.20, f32[1,512]{1,0:T(1,128)S(1)} %get-tuple-element.50.gain, bf16[512,1536]{1,0:T(8,128)(2,1)S(1)} %get-tuple-element.51.attend, f32[1,8]{1,0:T(1,128)S(1)} %get-tuple-element.52.scale, ...), custom_call_target="tpu_custom_call" | custom-call | tf_op jit(solution)/shard_map/pallas_call | solution.py:445
  44.7 16.8 %all_to_all.16 = bf16[64,4,128]{2,1,0:T(4,128)(2,1)S(1)} all-to-all(bf16[64,4,128]{2,1,0:T(4,128)(2,1)S(1)} %bitcast.23), channel_id=1, replica_groups=mesh['frames'=64,'rows'=8] {'frames'}, dimensions={0} | all-to-all | bytes 131072 | tf_op jit(solution)/shard_map/all_to_all | solution.py:574
  61.5 2.2 %shard_map.134 = (bf16[2048,128]{1,0:T(8,128)(2,1)S(1)}, bf16[2048,128]{1,0:T(8,128)(2,1)S(1)}, bf16[48,512]{1,0:T(8,128)(2,1)S(1)}, bf16[48,512]{1,0:T(8,128)(2...) custom-call(s32[1]{0:T(128)} %bitcast.core, ...), custom_call_target="tpu_custom_call" | custom-call | tf_op jit(solution)/shard_map/pallas_call | solution.py:445
  63.8 2.3 %collective-permute-start.4 = (bf16[2048,128]{1,0:T(8,128)(2,1)S(1)}, bf16[2048,128]{1,0:T(8,128)(2,1)S(1)}, u32[]{:S(2)}, u32[]{:S(2)}) collective-permute-start(bf16[2048,128]{1,0:T(8,128)(2,1)S(1)} %get-tuple-element.74), channel_id=1, source_target_pairs={{0,8},{8,0},{16,24},{24,16},{32,40},{40,32},{48,56},{56,48},{64,72... | collective-permute-start | bytes 1572872 | tf_op jit(solution)/shard_map/ppermute | solution.py:607
  66.1 1.5 %collective-permute-done.4.sent = bf16[2048,128]{1,0:T(8,128)(2,1)S(1)} collective-permute-done((bf16[2048,128]{1,0:T(8,128)(2,1)S(1)}, bf16[2048,128]{1,0:T(8,128)(2,1)S(1)}, u32[]{:S(2)}, u32[]{:S(2)}) %collective-permute-start.4) | collective-permute-done | bytes 524320 | tf_op jit(solution)/shard_map/ppermute | solution.py:607
  67.6 0.9 shard_map.136
  68.5 9.3 %all-to-all-start.2 = ((bf16[256,8,128]{2,1,0:T(8,128)(2,1)}), bf16[256,8,128]{2,1,0:T(8,128)(2,1)S(1)}, u32[]{:S(2)}, u32[]{:S(2)}) async-start(bf16[256,8,128]{2,1,0:T(8,128)(2,1)} %bitcast.17), calls=%async_computation.2 | async-start | bytes 1048576 | tf_op jit(solution)/shard_map/all_to_all | solution.py:635
  77.8 1.6 %collective-permute-start.2 = (bf16[48,512]{1,0:T(8,128)(2,1)S(1)}, bf16[48,512]{1,0:T(8,128)(2,1)S(1)}, u32[]{:S(2)}, u32[]{:S(2)}) collective-permute-start(bf16[48,512]{1,0:T(8,128)(2,1)S(1)} %get-tuple-element.66), channel_id=1, source_target_pairs={{0,1},{1,2},{2,3},{3,4},{4,5},{5,6},{6,7},{8,9},{9,10},{10,11},{11... | collective-permute-start | bytes 147464 | tf_op jit(solution)/shard_map/ppermute | solution.py:609
  79.4 1.3 %collective-permute-start.3 = (bf16[48,512]{1,0:T(8,128)(2,1)S(1)}, bf16[48,512]{1,0:T(8,128)(2,1)S(1)}, u32[]{:S(2)}, u32[]{:S(2)}) collective-permute-start(bf16[48,512]{1,0:T(8,128)(2,1)S(1)} %get-tuple-element.67), channel_id=1, source_target_pairs={{1,0},{2,1},{3,2},{4,3},{5,4},{6,5},{7,6},{9,8},{10,9},{11,10},{12... | collective-permute-start | bytes 147464 | tf_op jit(solution)/shard_map/ppermute | solution.py:608
  80.7 5.8 %collective-permute-done.2.from_above = bf16[48,512]{1,0:T(8,128)(2,1)S(1)} collective-permute-done((bf16[48,512]{1,0:T(8,128)(2,1)S(1)}, bf16[48,512]{1,0:T(8,128)(2,1)S(1)}, u32[]{:S(2)}, u32[]{:S(2)}) %collective-permute-start.2) | collective-permute-done | bytes 49184 | tf_op jit(solution)/shard_map/ppermute | solution.py:609
  86.5 2.6 %collective-permute-done.3.from_below = bf16[48,512]{1,0:T(8,128)(2,1)S(1)} collective-permute-done((bf16[48,512]{1,0:T(8,128)(2,1)S(1)}, bf16[48,512]{1,0:T(8,128)(2,1)S(1)}, u32[]{:S(2)}, u32[]{:S(2)}) %collective-permute-start.3) | collective-permute-done | bytes 49184 | tf_op jit(solution)/shard_map/ppermute | solution.py:608
  89.2 1.2 %shard_map.135 = (bf16[256,256]{1,0:T(8,128)(2,1)}, f32[8,128]{1,0:T(8,128)S(1)}) custom-call(bf16[48,512]{1,0:T(8,128)(2,1)S(1)} %collective-permute-done.2.from_above, bf16[48,512]{1,0:T(8,128)(2,1)S(1)} %collective-permute-done.3.from_below, bf16[256,256]{1,0:T(8,128)(2,1)S(1)} %get-tuple-element.68.ct_query, ...), custom_call_target="tpu_custom_call" | custom-call | flops 170000000 | bytes 2000000 | tf_op jit(solution)/shard_map/pallas_call | solution.py:445
  90.3 6.2 %all-to-all-done.2.shares = bf16[256,8,128]{2,1,0:T(8,128)(2,1)S(1)} async-done(((bf16[256,8,128]{2,1,0:T(8,128)(2,1)}), bf16[256,8,128]{2,1,0:T(8,128)(2,1)S(1)}, u32[]{:S(2)}, u32[]{:S(2)}) %all-to-all-start.2) | async-done | bytes 524320 | tf_op jit(solution)/shard_map/all_to_all | solution.py:635
  96.6 0.7 shard_map.137
Async XLA Ops:
  1.4 9.4 %collective-permute-start = (bf16[48,256]{1,0:T(8,128)(2,1)S(1)}, bf16[48,256]{1,0:T(8,128)(2,1)S(1)}, u32[]{:S(2)}, u32[]{:S(2)}) collective-permute-start(bf16[48,256]{1,0:T(8,128)(2,1)S(1)} %bitcast.27), channel_id=1, source_target_pairs={{1,2},{2,1},{3,4},{4,3},{5,6},{6,5},{9,10},{10,9},{11,12},{12,11},... | collective-permute-start | bytes 73736 | tf_op jit(solution)/shard_map/ppermute | solution.py:505
  2.1 8.7 %collective-permute-start.1 = (bf16[48,256]{1,0:T(8,128)(2,1)S(1)}, bf16[48,256]{1,0:T(8,128)(2,1)S(1)}, u32[]{:S(2)}, u32[]{:S(2)}) collective-permute-start(bf16[48,256]{1,0:T(8,128)(2,1)S(1)} %bitcast.26), channel_id=1, source_target_pairs={{0,1},{1,0},{2,3},{3,2},{4,5},{5,4},{6,7},{7,6},{8,9},{9,8},{10,11... | collective-permute-start | bytes 73736 | tf_op jit(solution)/shard_map/ppermute | solution.py:507
  63.8 3.8 %collective-permute-start.4 = (bf16[2048,128]{1,0:T(8,128)(2,1)S(1)}, bf16[2048,128]{1,0:T(8,128)(2,1)S(1)}, u32[]{:S(2)}, u32[]{:S(2)}) collective-permute-start(bf16[2048,128]{1,0:T(8,128)(2,1)S(1)} %get-tuple-element.74), channel_id=1, source_target_pairs={{0,8},{8,0},{16,24},{24,16},{32,40},{40,32},{48,56},{56,48},{64,72... | collective-permute-start | bytes 1572872 | tf_op jit(solution)/shard_map/ppermute | solution.py:607
  68.5 28.1 %all-to-all-start.2 = ((bf16[256,8,128]{2,1,0:T(8,128)(2,1)}), bf16[256,8,128]{2,1,0:T(8,128)(2,1)S(1)}, u32[]{:S(2)}, u32[]{:S(2)}) async-start(bf16[256,8,128]{2,1,0:T(8,128)(2,1)} %bitcast.17), calls=%async_computation.2 | async-start | bytes 1048576 | tf_op jit(solution)/shard_map/all_to_all | solution.py:635
  77.8 8.7 %collective-permute-start.2 = (bf16[48,512]{1,0:T(8,128)(2,1)S(1)}, bf16[48,512]{1,0:T(8,128)(2,1)S(1)}, u32[]{:S(2)}, u32[]{:S(2)}) collective-permute-start(bf16[48,512]{1,0:T(8,128)(2,1)S(1)} %get-tuple-element.66), channel_id=1, source_target_pairs={{0,1},{1,2},{2,3},{3,4},{4,5},{5,6},{6,7},{8,9},{9,10},{10,11},{11... | collective-permute-start | bytes 147464 | tf_op jit(solution)/shard_map/ppermute | solution.py:609
  79.4 9.7 %collective-permute-start.3 = (bf16[48,512]{1,0:T(8,128)(2,1)S(1)}, bf16[48,512]{1,0:T(8,128)(2,1)S(1)}, u32[]{:S(2)}, u32[]{:S(2)}) collective-permute-start(bf16[48,512]{1,0:T(8,128)(2,1)S(1)} %get-tuple-element.67), channel_id=1, source_target_pairs={{1,0},{2,1},{3,2},{4,3},{5,4},{6,5},{7,6},{9,8},{10,9},{11,10},{12... | collective-permute-start | bytes 147464 | tf_op jit(solution)/shard_map/ppermute | solution.py:608
